TPU v7x, 256 devices: a whole 4x4x8 slice. The times are simulated.
256 devices in a mesh: blk: 32 (over y_lo, z, core), head: 8 (over y_hi, x).
Axes of the slice: x: 4, y: 4 (y_hi: 2, y_lo: 2; y = y_hi * 2 + y_lo), z: 8, core: 2. Of those that a mesh axis runs over, the one named last changes fastest.
Arguments:
- queries: bfloat16 [32768, 2048], P(('blk', 'head')), may hold values from -4.5 to 4.5
- keys: bfloat16 [32768, 2048], P(('blk', 'head')), may hold values from -4.5 to 4.5
- values: bfloat16 [32768, 2048], P(('blk', 'head')), may hold values from -6 to 6
- grad_out: bfloat16 [32768, 2048], P(('blk', 'head')), may hold values from -6 to 6
- key_blocks: int32 [256, 16], P('blk'), may hold values from 0 to 255, as said below
- doc_lengths: int32 [8], replicated, may hold values from 1 to 8192, 32768 in all
Outputs:
- attended: bfloat16 [32768, 2048], P(('blk', 'head'))
- grad_queries: bfloat16 [32768, 2048], P(('blk', 'head'))
- grad_keys: bfloat16 [32768, 2048], P(('blk', 'head'))
- grad_values: bfloat16 [32768, 2048], P(('blk', 'head'))
Inputs may be any that keep to these rules, and one draw needn't show every extreme that they name: `key_blocks`: row b lists the key blocks of query block b: its first entry is b itself, every entry lies between b - 23 and b. `doc_lengths`: the lengths sum to 32768.
All inputs are finite; a program needn't handle non-finite values.
Results may differ from a plain program's by a relative error of at most 0.011.
Values may be sent and summed in bfloat16 or wider, within the bound.
No kernel may reach another device: no remote copies, remote signals or barrier semaphores. Data moves between devices by JAX's collectives and lax.ppermute only.
A program may use at most 128 MiB of HBM per device.

v0:
```python
import jax
import jax.numpy as jnp
from jax import lax
from jax.sharding import PartitionSpec as P

HD = 128
BLOCK = 128
KB = 16
WIN = 24


def from_behind(value, axis, steps):
    count = lax.axis_size(axis)
    first, last = (max(0, -steps), min(count, count - steps))
    return lax.ppermute(value, axis, [(source, source + steps) for source in range(first, last)])


def document_begin(positions, doc_lengths):
    doc_starts = jnp.cumsum(doc_lengths) - doc_lengths
    earlier = doc_starts[None, :] <= positions[:, None]
    return jnp.max(jnp.where(earlier, doc_starts[None, :], 0), axis=1)


def tile_mask(first_query, listed, doc_lengths, block_width):
    offsets = jnp.arange(block_width, dtype=jnp.int32)
    query_pos = first_query + offsets
    key_pos = (listed[:, None] * block_width + offsets[None, :]).reshape(-1)
    ordering = jnp.arange(listed.shape[0], dtype=jnp.int32)
    repeated = jnp.any(
        (listed[:, None] == listed[None, :]) & (ordering[:, None] > ordering[None, :]), axis=1
    )
    unseen = jnp.repeat(jnp.logical_not(repeated), block_width)
    starting = document_begin(query_pos, doc_lengths)
    return (
        (key_pos[None, :] <= query_pos[:, None])
        & (key_pos[None, :] >= starting[:, None])
        & unseen[None, :]
    )


def probabilities(scores, allowed):
    masked = jnp.where(allowed[None], scores, -1e30)
    row_peak = jnp.max(masked, axis=-1, keepdims=True)
    weights = jnp.where(allowed[None], jnp.exp(masked - row_peak), 0.0)
    return weights / jnp.sum(weights, axis=-1, keepdims=True)


def on_device(queries, keys, values, grad_out, key_blocks, doc_lengths):
    local_q, local_k, local_v, local_g = (
        lax.all_to_all(queries, "head", split_axis=1, concat_axis=0, tiled=True),
        lax.all_to_all(keys, "head", split_axis=1, concat_axis=0, tiled=True),
        lax.all_to_all(values, "head", split_axis=1, concat_axis=0, tiled=True),
        lax.all_to_all(grad_out, "head", split_axis=1, concat_axis=0, tiled=True),
    )
    row_count = local_q.shape[0]
    head_count = local_q.shape[1] // HD
    per_shard = row_count // BLOCK
    reach = (WIN - 2 + per_shard) // per_shard
    shard_index = lax.axis_index("blk")
    score_scale = HD ** (-0.5)
    pieces = [(local_k, local_v)]
    current = (local_k, local_v)
    for stride in range(reach):
        current = from_behind((current[0], current[1]), "blk", 1)
        pieces.append(current)
    window_count = (reach + 1) * per_shard
    tile_width = BLOCK * head_count * HD
    tile_shape = (-1, BLOCK, head_count, HD)
    window_keys = jnp.concatenate(
        [pieces[reach - slot][0] for slot in range(reach + 1)], axis=0
    ).reshape(window_count, tile_width)
    window_values = jnp.concatenate(
        [pieces[reach - slot][1] for slot in range(reach + 1)], axis=0
    ).reshape(window_count, tile_width)
    window_base = (shard_index - reach) * per_shard
    query_grid = local_q.reshape(tile_shape)
    grad_grid = local_g.reshape(tile_shape)
    block_ids = shard_index * per_shard + jnp.arange(per_shard, dtype=jnp.int32)
    window_ids = jnp.arange(window_count, dtype=jnp.int32)

    def gather_tiles(listed):
        selector = (listed - window_base)[:, None] == window_ids[None, :]
        chooser = selector.astype(jnp.bfloat16)
        key_tiles = jnp.dot(chooser, window_keys, preferred_element_type=jnp.float32).astype(
            jnp.bfloat16
        )
        value_tiles = jnp.dot(chooser, window_values, preferred_element_type=jnp.float32).astype(
            jnp.bfloat16
        )
        return (
            selector,
            key_tiles.reshape(KB * BLOCK, head_count, HD),
            value_tiles.reshape(KB * BLOCK, head_count, HD),
        )

    def forward(inputs):
        block_id, listed, query_tile = inputs
        selector, key_tiles, value_tiles = gather_tiles(listed)
        allowed = tile_mask(block_id * BLOCK, listed, doc_lengths, BLOCK)
        scores = (
            jnp.einsum("qhd,khd->hqk", query_tile, key_tiles, preferred_element_type=jnp.float32)
            * score_scale
        )
        rounded = probabilities(scores, allowed).astype(jnp.bfloat16)
        return jnp.einsum(
            "hqk,khd->qhd", rounded, value_tiles, preferred_element_type=jnp.float32
        ).astype(jnp.bfloat16)

    attended = lax.map(forward, (block_ids, key_blocks, query_grid))
    attended_rows = attended.reshape(row_count, head_count * HD)

    def backward(carried, inputs):
        key_sum, value_sum = carried
        block_id, listed, query_tile, gradient, output = inputs
        selector, key_tiles, value_tiles = gather_tiles(listed)
        allowed = tile_mask(block_id * BLOCK, listed, doc_lengths, BLOCK)
        scores = (
            jnp.einsum("qhd,khd->hqk", query_tile, key_tiles, preferred_element_type=jnp.float32)
            * score_scale
        )
        weights = probabilities(scores, allowed)
        rounded = weights.astype(jnp.bfloat16)
        row_delta = jnp.sum(gradient.astype(jnp.float32) * output.astype(jnp.float32), axis=-1).T
        dprobs = jnp.einsum(
            "qhd,khd->hqk", gradient, value_tiles, preferred_element_type=jnp.float32
        )
        dscores = (weights * (dprobs - row_delta[:, :, None])).astype(jnp.bfloat16)
        grad_query = (
            jnp.einsum("hqk,khd->qhd", dscores, key_tiles, preferred_element_type=jnp.float32)
            * score_scale
        ).astype(jnp.bfloat16)
        key_part = (
            jnp.einsum("hqk,qhd->khd", dscores, query_tile, preferred_element_type=jnp.float32)
            * score_scale
        )
        value_part = jnp.einsum(
            "hqk,qhd->khd", rounded, gradient, preferred_element_type=jnp.float32
        )
        placer = selector.astype(jnp.float32).T
        key_sum = key_sum + jnp.dot(
            placer,
            key_part.reshape(KB, tile_width),
            precision=lax.Precision.HIGHEST,
            preferred_element_type=jnp.float32,
        )
        value_sum = value_sum + jnp.dot(
            placer,
            value_part.reshape(KB, tile_width),
            precision=lax.Precision.HIGHEST,
            preferred_element_type=jnp.float32,
        )
        return ((key_sum, value_sum), grad_query)

    zero_sum = jnp.zeros((window_count, tile_width), jnp.float32)
    sums, grad_blocks = lax.scan(
        backward, (zero_sum, zero_sum), (block_ids, key_blocks, query_grid, grad_grid, attended)
    )
    key_parts = sums[0].reshape(reach + 1, row_count, head_count * HD)
    value_parts = sums[1].reshape(reach + 1, row_count, head_count * HD)
    summed = (key_parts[0], value_parts[0])
    for stride in range(1, reach + 1):
        arrived = from_behind((summed[0], summed[1]), "blk", -1)
        summed = (arrived[0] + key_parts[stride], arrived[1] + value_parts[stride])
    grad_q_rows = grad_blocks.reshape(row_count, head_count * HD)
    grad_k_rows = summed[0].astype(jnp.bfloat16)
    grad_v_rows = summed[1].astype(jnp.bfloat16)
    back_out, back_q, back_k, back_v = (
        lax.all_to_all(attended_rows, "head", split_axis=0, concat_axis=1, tiled=True),
        lax.all_to_all(grad_q_rows, "head", split_axis=0, concat_axis=1, tiled=True),
        lax.all_to_all(grad_k_rows, "head", split_axis=0, concat_axis=1, tiled=True),
        lax.all_to_all(grad_v_rows, "head", split_axis=0, concat_axis=1, tiled=True),
    )
    return (back_out, back_q, back_k, back_v)


def solution(mesh):
    placed = (
        P(("blk", "head"), None),
        P(("blk", "head"), None),
        P(("blk", "head"), None),
        P(("blk", "head"), None),
        P("blk", None),
        P(),
    )
    return jax.shard_map(
        on_device,
        mesh=mesh,
        in_specs=placed,
        out_specs=(
            P(("blk", "head"), None),
            P(("blk", "head"), None),
            P(("blk", "head"), None),
            P(("blk", "head"), None),
        ),
        check_vma=False,
    )
```

profile of v0, /device:TPU:232, one launch (start us, length us, event | category | flops | bytes accessed | tf_op | source)
XLA Modules:
  0.0 783.3 jit_solution(14071567122897006096)
XLA Ops:
  3.0 6.2 all-to-all-start
  10.5 10.3 %all-to-all-done = bf16[128,8,256]{2,0,1:T(8,128)(2,1)S(1)} async-done(((bf16[128,8,256]{2,0,1:T(8,128)(2,1)}), bf16[128,8,256]{2,0,1:T(8,128)(2,1)S(1)}, u32[]{:S(2)}, u32[]{:S(2)}) %all-to-all-start) | async-done | bytes 524320 | tf_op jit(solution)/shard_map/all_to_all | solution.py:52
  26.2 9.7 %all-to-all-done.2 = bf16[128,8,256]{2,0,1:T(8,128)(2,1)S(1)} async-done(((bf16[128,8,256]{2,0,1:T(8,128)(2,1)}), bf16[128,8,256]{2,0,1:T(8,128)(2,1)S(1)}, u32[]{:S(2)}, u32[]{:S(2)}) %all-to-all-start.2) | async-done | bytes 524320 | tf_op jit(solution)/shard_map/all_to_all | solution.py:51
  39.8 6.6 collective-permute-done.3
  61.8 9.3 %all-to-all-done.1 = bf16[128,8,256]{0,2,1:T(8,128)(2,1)S(1)} async-done(((bf16[128,8,256]{0,2,1:T(8,128)(2,1)}), bf16[128,8,256]{0,2,1:T(8,128)(2,1)S(1)}, u32[]{:S(2)}, u32[]{:S(2)}) %all-to-all-start.1) | async-done | bytes 524320 | tf_op jit(solution)/shard_map/all_to_all | solution.py:50
  84.5 4.3 reshape.393
  89.7 122.2 %while.30 = (s32[]{:T(128)}, bf16[8,128,2,128]{1,3,2,0:T(8,128)(2,1)}, s32[8,16]{1,0:T(8,128)}, s32[]{:T(128)}, bf16[32,32768]{1,0:T(8,128)(2,1)S(1)}, /*index=5...) while((s32[]{:T(128)}, ...), condition=%wide.region_6.7_spmd.clone, body=%wide.region_1.6_spmd.clone.sunk | while | flops 341353504 | bytes 17720640 | solution.py:109
  212.8 431.4 %while.31 = (s32[]{:T(128)}, f32[32,32768]{1,0:T(8,128)}, f32[32,32768]{1,0:T(8,128)}, bf16[8,128,2,128]{1,3,2,0:T(8,128)(2,1)}, s32[8,16]{1,0:T(8,128)}, /*inde...) while((s32[]{:T(128)}, f32[32,32768]{1,0:T(8,128)}, ...), condition=%wide.region_13.14_spmd.clone, body=%wide.region_7.13_spmd.clone.sunk | while | flops 1153640192 | bytes 127627960 | solution.py:155
  236.2 4.2 copy.176
  255.0 5.7 convolution_add_fusion.4
  289.1 4.2 copy.176
  307.9 7.0 convolution_add_fusion.4
  343.2 4.2 copy.176
  361.9 7.0 convolution_add_fusion.4
  397.2 4.2 copy.176
  416.0 7.0 convolution_add_fusion.4
  451.3 4.2 copy.176
  470.1 7.0 convolution_add_fusion.4
  505.4 4.2 copy.176
  524.2 7.0 convolution_add_fusion.4
  559.5 4.2 copy.176
  578.3 7.0 convolution_add_fusion.4
  613.6 4.2 copy.176
  632.3 7.0 convolution_add_fusion.4
  644.2 5.8 fusion.87
  662.3 5.6 collective-permute-done.6
  698.9 6.8 all-to-all-start.3
  712.5 22.5 %all-to-all-done.3 = bf16[8,128,256]{2,1,0:T(8,128)(2,1)} async-done(((bf16[8,128,256]{2,1,0:T(8,128)(2,1)}), bf16[8,128,256]{2,1,0:T(8,128)(2,1)}, u32[]{:S(2)}, u32[]{:S(2)}) %all-to-all-start.3) | async-done | bytes 524320 | tf_op jit(solution)/shard_map/all_to_all | solution.py:168
  735.0 4.8 all-to-all-start.5
  742.2 9.6 %all-to-all-done.5 = bf16[8,128,256]{2,1,0:T(8,128)(2,1)} async-done(((bf16[8,128,256]{2,1,0:T(8,128)(2,1)}), bf16[8,128,256]{2,1,0:T(8,128)(2,1)}, u32[]{:S(2)}, u32[]{:S(2)}) %all-to-all-start.5) | async-done | bytes 524320 | tf_op jit(solution)/shard_map/all_to_all | solution.py:169
  757.5 9.4 %all-to-all-done.6 = bf16[8,128,256]{2,1,0:T(8,128)(2,1)S(1)} async-done(((bf16[8,128,256]{2,1,0:T(8,128)(2,1)}), bf16[8,128,256]{2,1,0:T(8,128)(2,1)S(1)}, u32[]{:S(2)}, u32[]{:S(2)}) %all-to-all-start.6) | async-done | bytes 524320 | tf_op jit(solution)/shard_map/all_to_all | solution.py:170
  776.4 5.7 all-to-all-done.7
  (531 shorter events, 566.4 us)
Async XLA Ops:
  0.6 8.6 %copy-start.6 = (bf16[128,2048]{1,0:T(8,128)(2,1)S(1)}, bf16[128,2048]{1,0:T(8,128)(2,1)}, u32[]{:S(2)}) copy-start(bf16[128,2048]{1,0:T(8,128)(2,1)} %param.11) | copy-start | bytes 1572868
  3.0 51.0 %copy-start.7 = (bf16[128,2048]{1,0:T(8,128)(2,1)S(1)}, bf16[128,2048]{1,0:T(8,128)(2,1)}, u32[]{:S(2)}) copy-start(bf16[128,2048]{1,0:T(8,128)(2,1)} %param.10) | copy-start | bytes 1572868
  3.0 17.8 %all-to-all-start = ((bf16[128,8,256]{2,0,1:T(8,128)(2,1)}), bf16[128,8,256]{2,0,1:T(8,128)(2,1)S(1)}, u32[]{:S(2)}, u32[]{:S(2)}) async-start(bf16[128,8,256]{2,0,1:T(8,128)(2,1)} %copy.124), calls=%async_computation | async-start | bytes 1048576 | tf_op jit(solution)/shard_map/all_to_all | solution.py:52
  9.5 49.1 %copy-start.11 = (s32[8]{0:T(128)S(1)}, s32[8]{0:T(128)}, u32[]{:S(2)}) copy-start(s32[8]{0:T(128)} %param.15) | copy-start | bytes 100
  9.5 51.3 %copy-start.8 = (bf16[128,2048]{1,0:T(8,128)(2,1)S(1)}, bf16[128,2048]{1,0:T(8,128)(2,1)}, u32[]{:S(2)}) copy-start(bf16[128,2048]{1,0:T(8,128)(2,1)} %param.13) | copy-start | bytes 1572868
  20.8 15.1 %all-to-all-start.2 = ((bf16[128,8,256]{2,0,1:T(8,128)(2,1)}), bf16[128,8,256]{2,0,1:T(8,128)(2,1)S(1)}, u32[]{:S(2)}, u32[]{:S(2)}) async-start(bf16[128,8,256]{2,0,1:T(8,128)(2,1)} %copy.127), calls=%async_computation.2 | async-start | bytes 1048576 | tf_op jit(solution)/shard_map/all_to_all | solution.py:51
  24.3 13.6 %collective-permute-start = (bf16[1024,256]{1,0:T(8,128)(2,1)S(1)}, bf16[1024,256]{1,0:T(8,128)(2,1)S(1)}, u32[]{:S(2)}, u32[]{:S(2)}) collective-permute-start(bf16[1024,256]{1,0:T(8,128)(2,1)S(1)} %bitcast.186), channel_id=1, source_target_pairs={{0,8},{8,16},{16,24},{24,32},{32,40},{40,48},{48,56},{56,64},{64,7... | collective-permute-start | bytes 1572872 | tf_op jit(solution)/shard_map/ppermute | solution.py:15
  35.9 10.5 %collective-permute-start.3 = (bf16[1024,256]{1,0:T(8,128)(2,1)S(1)}, bf16[1024,256]{1,0:T(8,128)(2,1)S(1)}, u32[]{:S(2)}, u32[]{:S(2)}) collective-permute-start(bf16[1024,256]{1,0:T(8,128)(2,1)S(1)} %bitcast.188), channel_id=1, source_target_pairs={{0,8},{8,16},{16,24},{24,32},{32,40},{40,48},{48,56},{56,64},{64,7... | collective-permute-start | bytes 1572872 | tf_op jit(solution)/shard_map/ppermute | solution.py:15
  37.8 17.2 %copy-start.9 = (bf16[1024,256]{1,0:T(8,128)(2,1)}, bf16[1024,256]{1,0:T(8,128)(2,1)S(1)}, u32[]{:S(2)}) copy-start(bf16[1024,256]{1,0:T(8,128)(2,1)S(1)} %collective-permute-done) | copy-start | bytes 1572868
  37.9 14.3 %collective-permute-start.1 = (bf16[1024,256]{1,0:T(8,128)(2,1)S(1)}, bf16[1024,256]{1,0:T(8,128)(2,1)}, u32[]{:S(2)}, u32[]{:S(2)}) collective-permute-start(bf16[1024,256]{1,0:T(8,128)(2,1)S(1)} %collective-permute-done), channel_id=1, source_target_pairs={{0,8},{8,16},{16,24},{24,32},{32,40},{40,48},{48,56},{56,64},{64,7... | collective-permute-start | bytes 1572872 | tf_op jit(solution)/shard_map/ppermute | solution.py:15
  46.4 12.4 %collective-permute-start.4 = (bf16[1024,256]{1,0:T(8,128)(2,1)S(1)}, bf16[1024,256]{1,0:T(8,128)(2,1)}, u32[]{:S(2)}, u32[]{:S(2)}) collective-permute-start(bf16[1024,256]{1,0:T(8,128)(2,1)S(1)} %collective-permute-done.3), channel_id=1, source_target_pairs={{0,8},{8,16},{16,24},{24,32},{32,40},{40,48},{48,56},{56,64},{64,7... | collective-permute-start | bytes 1572872 | tf_op jit(solution)/shard_map/ppermute | solution.py:15
  52.1 24.1 %collective-permute-start.2 = (bf16[1024,256]{1,0:T(8,128)(2,1)}, bf16[1024,256]{1,0:T(8,128)(2,1)}, u32[]{:S(2)}, u32[]{:S(2)}) collective-permute-start(bf16[1024,256]{1,0:T(8,128)(2,1)} %collective-permute-done.1), channel_id=1, source_target_pairs={{0,8},{8,16},{16,24},{24,32},{32,40},{40,48},{48,56},{56,64},{64,7... | collective-permute-start | bytes 1572872 | tf_op jit(solution)/shard_map/ppermute | solution.py:15
  55.1 16.0 %all-to-all-start.1 = ((bf16[128,8,256]{0,2,1:T(8,128)(2,1)}), bf16[128,8,256]{0,2,1:T(8,128)(2,1)S(1)}, u32[]{:S(2)}, u32[]{:S(2)}) async-start(bf16[128,8,256]{0,2,1:T(8,128)(2,1)} %bitcast.6), calls=%async_computation.1 | async-start | bytes 1048576 | tf_op jit(solution)/shard_map/all_to_all | solution.py:50
  58.6 17.7 %copy-start.10 = (bf16[1024,256]{1,0:T(8,128)(2,1)S(1)}, bf16[1024,256]{1,0:T(8,128)(2,1)}, u32[]{:S(2)}) copy-start(bf16[1024,256]{1,0:T(8,128)(2,1)} %copy-done.9) | copy-start | bytes 1572868
  58.8 23.1 %collective-permute-start.5 = (bf16[1024,256]{1,0:T(8,128)(2,1)}, bf16[1024,256]{1,0:T(8,128)(2,1)}, u32[]{:S(2)}, u32[]{:S(2)}) collective-permute-start(bf16[1024,256]{1,0:T(8,128)(2,1)} %collective-permute-done.4), channel_id=1, source_target_pairs={{0,8},{8,16},{16,24},{24,32},{32,40},{40,48},{48,56},{56,64},{64,7... | collective-permute-start | bytes 1572872 | tf_op jit(solution)/shard_map/ppermute | solution.py:15
  71.0 140.8 %all-to-all-start.4 = ((bf16[128,8,256]{0,2,1:T(8,128)(2,1)}), bf16[128,8,256]{0,2,1:T(8,128)(2,1)}, u32[]{:S(2)}, u32[]{:S(2)}) async-start(bf16[128,8,256]{0,2,1:T(8,128)(2,1)} %bitcast.16), calls=%async_computation.4 | async-start | bytes 1048576 | tf_op jit(solution)/shard_map/all_to_all | solution.py:53
  307.9 7.0 copy-start.1
  361.9 7.0 copy-start.1
  416.0 7.0 copy-start.1
  470.1 7.0 copy-start.1
  524.2 7.0 copy-start.1
  578.3 7.0 copy-start.1
  652.4 15.5 %collective-permute-start.6 = (f32[1024,256]{1,0:T(8,128)}, f32[1024,256]{1,0:T(8,128)}, u32[]{:S(2)}, u32[]{:S(2)}) collective-permute-start(f32[1024,256]{1,0:T(8,128)} %squeeze.57), channel_id=1, source_target_pairs={{8,0},{16,8},{24,16},{32,24},{40,32},{48,40},{56,48},{64,56},{72,6... | collective-permute-start | bytes 3145736 | tf_op jit(solution)/shard_map/ppermute | solution.py:15
  657.7 21.5 %collective-permute-start.9 = (f32[1024,256]{1,0:T(8,128)}, f32[1024,256]{1,0:T(8,128)}, u32[]{:S(2)}, u32[]{:S(2)}) collective-permute-start(f32[1024,256]{1,0:T(8,128)} %squeeze.61), channel_id=1, source_target_pairs={{8,0},{16,8},{24,16},{32,24},{40,32},{48,40},{56,48},{64,56},{72,6... | collective-permute-start | bytes 3145736 | tf_op jit(solution)/shard_map/ppermute | solution.py:15
  670.6 19.8 %collective-permute-start.7 = (f32[1024,256]{1,0:T(8,128)}, f32[1024,256]{1,0:T(8,128)}, u32[]{:S(2)}, u32[]{:S(2)}) collective-permute-start(f32[1024,256]{1,0:T(8,128)} %add.117), channel_id=1, source_target_pairs={{8,0},{16,8},{24,16},{32,24},{40,32},{48,40},{56,48},{64,56},{72,6... | collective-permute-start | bytes 3145736 | tf_op jit(solution)/shard_map/ppermute | solution.py:15
  681.8 25.0 %collective-permute-start.10 = (f32[1024,256]{1,0:T(8,128)}, f32[1024,256]{1,0:T(8,128)}, u32[]{:S(2)}, u32[]{:S(2)}) collective-permute-start(f32[1024,256]{1,0:T(8,128)} %add.120), channel_id=1, source_target_pairs={{8,0},{16,8},{24,16},{32,24},{40,32},{48,40},{56,48},{64,56},{72,6... | collective-permute-start | bytes 3145736 | tf_op jit(solution)/shard_map/ppermute | solution.py:15
  693.1 47.0 %collective-permute-start.8 = (f32[1024,256]{1,0:T(8,128)}, f32[1024,256]{1,0:T(8,128)}, u32[]{:S(2)}, u32[]{:S(2)}) collective-permute-start(f32[1024,256]{1,0:T(8,128)} %add.118), channel_id=1, source_target_pairs={{8,0},{16,8},{24,16},{32,24},{40,32},{48,40},{56,48},{64,56},{72,6... | collective-permute-start | bytes 3145736 | tf_op jit(solution)/shard_map/ppermute | solution.py:15
  698.9 36.1 %all-to-all-start.3 = ((bf16[8,128,256]{2,1,0:T(8,128)(2,1)}), bf16[8,128,256]{2,1,0:T(8,128)(2,1)}, u32[]{:S(2)}, u32[]{:S(2)}) async-start(bf16[8,128,256]{2,1,0:T(8,128)(2,1)} %copy.145), calls=%async_computation.3 | async-start | bytes 1048576 | tf_op jit(solution)/shard_map/all_to_all | solution.py:168
  709.6 45.8 %collective-permute-start.11 = (f32[1024,256]{1,0:T(8,128)}, f32[1024,256]{1,0:T(8,128)}, u32[]{:S(2)}, u32[]{:S(2)}) collective-permute-start(f32[1024,256]{1,0:T(8,128)} %add.121), channel_id=1, source_target_pairs={{8,0},{16,8},{24,16},{32,24},{40,32},{48,40},{56,48},{64,56},{72,6... | collective-permute-start | bytes 3145736 | tf_op jit(solution)/shard_map/ppermute | solution.py:15
  735.0 16.7 %all-to-all-start.5 = ((bf16[8,128,256]{2,1,0:T(8,128)(2,1)}), bf16[8,128,256]{2,1,0:T(8,128)(2,1)}, u32[]{:S(2)}, u32[]{:S(2)}) async-start(bf16[8,128,256]{2,1,0:T(8,128)(2,1)} %copy.146), calls=%async_computation.5 | async-start | bytes 1048576 | tf_op jit(solution)/shard_map/all_to_all | solution.py:169
  751.7 15.2 %all-to-all-start.6 = ((bf16[8,128,256]{2,1,0:T(8,128)(2,1)}), bf16[8,128,256]{2,1,0:T(8,128)(2,1)S(1)}, u32[]{:S(2)}, u32[]{:S(2)}) async-start(bf16[8,128,256]{2,1,0:T(8,128)(2,1)} %bitcast.22), calls=%async_computation.6 | async-start | bytes 1048576 | tf_op jit(solution)/shard_map/all_to_all | solution.py:170
  766.9 15.2 %all-to-all-start.7 = ((bf16[8,128,256]{2,1,0:T(8,128)(2,1)}), bf16[8,128,256]{2,1,0:T(8,128)(2,1)S(1)}, u32[]{:S(2)}, u32[]{:S(2)}) async-start(bf16[8,128,256]{2,1,0:T(8,128)(2,1)} %bitcast.25), calls=%async_computation.7 | async-start | bytes 1048576 | tf_op jit(solution)/shard_map/all_to_all | solution.py:171
  (43 other events, 153.9 us)
where the time goes:
time: 790 us; the launch traced here: 783 us
  local copies, waits for them, and re-layouts  291 us (37%)
  matrix products  273 us (35%)
  waiting for transfers between devices  97.3 us (12%)
  starting transfers between devices  66 us (8%)
  other arithmetic  43.4 us (5%)
  loops' own time  11.5 us (1%)
    sub x16, matrix products, probabilities(): weights = jnp.where(allowed[None], jnp.exp(masked - row_peak), 0.0)  56 us
    dot_general x8, matrix products, backward(): jnp.dot(placer, key_part.reshape(KB, tile_width), precision=lax.Precision...  54.5 us
    reshape x24, local copies, waits for them, and re-layouts, gather_tiles(): key_tiles.reshape(KB * BLOCK, head_count, HD)  44.6 us
    transpose x8, local copies, waits for them, and re-layouts, backward(): jnp.einsum('hqk,qhd->khd', rounded, gradient, preferred_element_type=jnp....  33.4 us
    reshape x16, local copies, waits for them, and re-layouts, gather_tiles(): value_tiles.reshape(KB * BLOCK, head_count, HD)  33.3 us
    dot_general x16, matrix products, gather_tiles(): jnp.dot(chooser, window_keys, preferred_element_type=jnp.float32)  33.2 us
    mul x8, local copies, waits for them, and re-layouts, backward(): jnp.einsum('hqk,qhd->khd', dscores, query_tile, preferred_element_type=jn...  33 us
    reshape x8, local copies, waits for them, and re-layouts, backward(): value_part.reshape(KB, tile_width)  31.4 us
  transfers between devices with their start and end apart: 20, of which 12 were waited for; matrix products, arithmetic and copies ran while one was open for 22% of the time, Pallas kernels for 0%

commit v1 on v0

v1 whole, which is shorter than its diff:
```python
import functools
import math

import jax
import jax.numpy as jnp
from jax import lax
from jax.experimental import pallas as pl
from jax.experimental.pallas import tpu as pltpu
from jax.sharding import Mesh
from jax.sharding import PartitionSpec as P

HD = 128
BLOCK = 128
KB = 16
WIN = 24
SCALE = HD**-0.5
LOG2E = math.log2(math.e)
GROUP = 4
CORES = ("core", "head")
NN = (((1,), (0,)), ((), ()))
TN = (((0,), (0,)), ((), ()))


def dot(a, b, dims):
    return lax.dot_general(a, b, dims, preferred_element_type=jnp.float32)


def fold(x, op):
    return op(x.reshape(BLOCK // 8, 8, BLOCK), axis=0)


def attend_kernel(
    unroll, tile_ref, start_ref, doc_ref, qg_ref, kv0_ref, kv1_ref, kv2_ref,
    out_ref, own_ref, prev_ref, far_ref, kv, acc, s_buf, d_buf, sems,
):
    far, per = far_ref.shape[0], qg_ref.shape[0]
    copies = [
        pltpu.make_async_copy(kv2_ref, kv.at[pl.ds(0, far)], sems.at[0]),
        pltpu.make_async_copy(kv1_ref, kv.at[pl.ds(far, per)], sems.at[1]),
        pltpu.make_async_copy(kv0_ref, kv.at[pl.ds(far + per, per)], sems.at[2]),
    ]
    for copy in copies:
        copy.start()
    acc[...] = jnp.zeros_like(acc)
    docs, total = [], jnp.int32(0)
    for d in range(doc_ref.shape[0]):
        docs.append(total)
        total = total + doc_ref[d]
    sub = lax.broadcasted_iota(jnp.int32, (BLOCK, BLOCK), 0)
    lane = lax.broadcasted_iota(jnp.int32, (BLOCK, BLOCK), 1)
    lane_row = lax.broadcasted_iota(jnp.int32, (1, BLOCK), 1)
    for copy in copies:
        copy.wait()

    def one(t, slot):
        s_ref, d_ref = s_buf.at[slot], d_buf.at[slot]
        q, g = qg_ref[t, 0], qg_ref[t, 1]
        qt, gt = q.T, g.T
        tiles = [tile_ref[t, i] for i in range(KB)]
        query_pos = start_ref[t, 0] + lane_row
        begin = jnp.zeros((1, BLOCK), jnp.int32)
        for first in docs:
            begin = jnp.where(first <= query_pos, first, begin)
        peak = jnp.full((8, BLOCK), -3e38, jnp.float32)
        for j in range(0, KB, GROUP):
            k_rows = jnp.concatenate([kv[tiles[i], 0] for i in range(j, j + GROUP)], axis=0)
            scores = dot(k_rows, qt, NN)
            for i in range(j, j + GROUP):
                s = scores[(i - j) * BLOCK : (i - j + 1) * BLOCK]
                allowed = sub >= begin - start_ref[t, i]
                if i == 0:
                    allowed = allowed & (sub <= lane)
                s = jnp.where(allowed, s, -1e30)
                s_ref[i] = s
                peak = jnp.maximum(peak, fold(s, jnp.max))
        for j in range(0, KB, GROUP):
            v_rows = jnp.concatenate([kv[tiles[i], 1] for i in range(j, j + GROUP)], axis=0)
            d_ref[pl.ds(j, GROUP)] = dot(v_rows, gt, NN).reshape(GROUP, BLOCK, BLOCK)
        c = SCALE * LOG2E
        peak = jnp.max(peak, axis=0, keepdims=True) * c
        sum_p = jnp.zeros((8, BLOCK), jnp.float32)
        sum_d = jnp.zeros((8, BLOCK), jnp.float32)
        for i in range(KB):
            p = jnp.exp2(s_ref[i] * c - peak)
            s_ref[i] = p
            sum_p = sum_p + fold(p, jnp.sum)
            sum_d = sum_d + fold(p * d_ref[i], jnp.sum)
        inv = 1.0 / jnp.sum(sum_p, axis=0, keepdims=True)
        delta = jnp.sum(sum_d, axis=0, keepdims=True) * inv
        attended = jnp.zeros((BLOCK, HD), jnp.float32)
        grad_q = jnp.zeros((BLOCK, HD), jnp.float32)
        for j in range(0, KB, GROUP):
            group = range(j, j + GROUP)
            p = [s_ref[i] * inv for i in group]
            p_low = jnp.concatenate([x.astype(jnp.bfloat16) for x in p], axis=0)
            ds = jnp.concatenate(
                [(p[i - j] * (d_ref[i] - delta)).astype(jnp.bfloat16) for i in group], axis=0
            )
            dv = dot(p_low, g, NN)
            for i in group:
                acc[tiles[i], 1] += dv[(i - j) * BLOCK : (i - j + 1) * BLOCK]
            dk = dot(ds, q, NN)
            for i in group:
                acc[tiles[i], 0] += dk[(i - j) * BLOCK : (i - j + 1) * BLOCK]
            attended += dot(p_low, jnp.concatenate([kv[tiles[i], 1] for i in group], axis=0), TN)
            grad_q += dot(ds, jnp.concatenate([kv[tiles[i], 0] for i in group], axis=0), TN)
        out_ref[t, 0] = attended.astype(jnp.bfloat16)
        out_ref[t, 1] = (grad_q * SCALE).astype(jnp.bfloat16)

    def step(t, _):
        for u in range(unroll):
            one(t * unroll + u, u)
        return 0

    lax.fori_loop(0, per // unroll, step, 0)
    far_ref[:, 0] = (acc[:far, 0] * SCALE).astype(jnp.bfloat16)
    far_ref[:, 1] = acc[:far, 1].astype(jnp.bfloat16)
    prev_ref[:, 0] = (acc[far : far + per, 0] * SCALE).astype(jnp.bfloat16)
    prev_ref[:, 1] = acc[far : far + per, 1].astype(jnp.bfloat16)
    own_ref[:, 0] = acc[far + per :, 0] * SCALE
    own_ref[:, 1] = acc[far + per :, 1]


def attend(tiles, starts, docs, qg, kv0, kv1, kv2, unroll):
    per, far = qg.shape[0], kv2.shape[0]
    smem = pl.BlockSpec(memory_space=pltpu.SMEM)
    vmem = pl.BlockSpec(memory_space=pltpu.VMEM)
    anywhere = pl.BlockSpec(memory_space=pl.ANY)

    def blocks(count, kind):
        return jax.ShapeDtypeStruct((count, 2, BLOCK, HD), kind)

    return pl.pallas_call(
        functools.partial(attend_kernel, unroll),
        out_shape=(
            blocks(per, jnp.bfloat16),
            blocks(per, jnp.float32),
            blocks(per, jnp.bfloat16),
            blocks(far, jnp.bfloat16),
        ),
        in_specs=[smem, smem, smem, vmem, anywhere, anywhere, anywhere],
        out_specs=(vmem,) * 4,
        scratch_shapes=[
            pltpu.VMEM((far + 2 * per, 2, BLOCK, HD), jnp.bfloat16),
            pltpu.VMEM((far + 2 * per, 2, BLOCK, HD), jnp.float32),
            pltpu.VMEM((unroll, KB, BLOCK, BLOCK), jnp.float32),
            pltpu.VMEM((unroll, KB, BLOCK, BLOCK), jnp.float32),
            pltpu.SemaphoreType.DMA((3,)),
        ],
        compiler_params=pltpu.CompilerParams(vmem_limit_bytes=48 << 20),
        cost_estimate=pl.CostEstimate(
            flops=12 * BLOCK * BLOCK * HD * KB * per,
            bytes_accessed=12 << 20,
            transcendentals=KB * per * BLOCK * BLOCK,
        ),
        name="attend",
    )(tiles, starts, docs, qg, kv0, kv1, kv2)


def shift(value, steps):
    count = lax.axis_size("yz")
    first, last = max(0, -steps), min(count, count - steps)
    return lax.ppermute(value, "yz", [(source, source + steps) for source in range(first, last)])


def to_heads(a, b):
    heads = a.shape[1] // HD
    pair = jnp.stack([a.reshape(BLOCK, heads, HD), b.reshape(BLOCK, heads, HD)])
    return lax.all_to_all(pair.transpose(2, 0, 1, 3), CORES, 0, 0, tiled=True)


def to_tokens(pair):
    pair = lax.all_to_all(pair, CORES, 0, 0, tiled=True)
    rows = pair.transpose(1, 2, 0, 3).reshape(2, BLOCK, -1)
    return rows[0], rows[1]


def on_device(queries, keys, values, grad_out, key_blocks, doc_lengths):
    per = lax.axis_size("core") * lax.axis_size("head")
    far = WIN - 1 - per
    partner = lax.ppermute(key_blocks, "core", [(0, 1), (1, 0)])
    is_first = lax.axis_index("core") == 0
    listed = jnp.concatenate(
        [jnp.where(is_first, key_blocks, partner), jnp.where(is_first, partner, key_blocks)]
    )
    order = jnp.arange(KB)
    repeated = jnp.any(
        (listed[:, :, None] == listed[:, None, :]) & (order[:, None] > order[None, :]), axis=2
    )
    tiles = listed - (lax.axis_index("yz") * per - (far + per))
    starts = jnp.where(repeated, -(1 << 30), listed * BLOCK)

    kv0 = to_heads(keys, values)
    kv1 = shift(kv0, 1)
    qg = to_heads(queries, grad_out)
    kv2 = shift(kv1[per - far :], 1)
    out, own, prev, last = attend(tiles, starts, doc_lengths, qg, kv0, kv1, kv2, 2)
    last = shift(last, -1)
    near = shift(prev[: per - far], -1)
    rest = prev[per - far :].astype(jnp.float32) + last.astype(jnp.float32)
    rest = shift(rest.astype(jnp.bfloat16), -1)
    attended, grad_q = to_tokens(out)
    grads = own + jnp.concatenate([near, rest]).astype(jnp.float32)
    grad_k, grad_v = to_tokens(grads.astype(jnp.bfloat16))
    return attended, grad_q, grad_k, grad_v


def solution(mesh):
    blk, head = mesh.devices.shape
    grid = Mesh(mesh.devices.reshape(blk // 2, 2, head), ("yz", "core", "head"))
    rows = P(("yz", "core", "head"), None)
    return jax.shard_map(
        on_device,
        mesh=grid,
        in_specs=(rows, rows, rows, rows, P(("yz", "core"), None), P()),
        out_specs=(rows,) * 4,
        check_vma=False,
    )
```

time: 790 us -> 180 us (0.23)
  the two profiles are of different devices: /device:TPU:232 before, /device:TPU:41 now
where the time goes in v1:
time: 180 us; the launch traced here: 177 us
  waiting for transfers between devices  68.2 us (38%)
  starting transfers between devices  38.2 us (21%)
  Pallas kernels  25.3 us (14%)
  blocking collectives  24.4 us (14%)
  local copies, waits for them, and re-layouts  15.4 us (9%)
  other arithmetic  4.18 us (2%)
    ppermute x5, waiting for transfers between devices, shift(): lax.ppermute(value, 'yz', [(source, source + steps) for source in range(f...  53.2 us
    pallas_call x1, Pallas kernels, attend(): pl.pallas_call(functools.partial(attend_kernel, unroll), out_shape=(block...  25.3 us
    all_to_all x1, blocking collectives, to_heads(): return lax.all_to_all(pair.transpose(2, 0, 1, 3), CORES, 0, 0, tiled=True)  24.4 us
    ppermute x5, starting transfers between devices, shift(): lax.ppermute(value, 'yz', [(source, source + steps) for source in range(f...  20.7 us
    all_to_all x2, waiting for transfers between devices, to_tokens(): pair = lax.all_to_all(pair, CORES, 0, 0, tiled=True)  15 us
    all_to_all x2, starting transfers between devices, to_tokens(): pair = lax.all_to_all(pair, CORES, 0, 0, tiled=True)  13.3 us
    unnamed x26, local copies, waits for them, and re-layouts  11.3 us
    all_to_all x1, starting transfers between devices, to_heads(): return lax.all_to_all(pair.transpose(2, 0, 1, 3), CORES, 0, 0, tiled=True)  3.98 us
  transfers between devices with their start and end apart: 9, of which 6 were waited for; matrix products, arithmetic and copies ran while one was open for 6% of the time, Pallas kernels for 0%

profile of v1, /device:TPU:41, one launch (start us, length us, event | category | flops | bytes accessed | tf_op | source)
XLA Modules:
  0.0 176.5 jit_solution(14875857145253342934)
XLA Ops:
  0.6 1.4 copy.30
  3.0 24.4 %all_to_all.20.kv0_ref = bf16[16,2,128,128]{3,2,1,0:T(8,128)(2,1)S(1)} all-to-all(bf16[16,2,128,128]{3,2,1,0:T(8,128)(2,1)S(1)} %maximum_bitcast_fusion.1), channel_id=1, replica_groups=mesh['yz'=16,'core'=2,'head'=8] {'core','head'}, dimensions={0} | all-to-all | bytes 2097152 | tf_op jit(solution)/shard_map/all_to_all | solution.py:169
  27.4 3.5 %collective-permute-start.1 = (bf16[16,2,128,128]{3,2,1,0:T(8,128)(2,1)S(1)}, bf16[16,2,128,128]{3,2,1,0:T(8,128)(2,1)S(1)}, u32[]{:S(2)}, u32[]{:S(2)}) collective-permute-start(bf16[16,2,128,128]{3,2,1,0:T(8,128)(2,1)S(1)} %all_to_all.20.kv0_ref), channel_id=1, source_target_pairs={{0,16},{16,32},{32,48},{48,64},{64,80},{80,96},{96,112},{112,128},... | collective-permute-start | bytes 3145736 | tf_op jit(solution)/shard_map/ppermute | solution.py:163
  31.3 0.3 copy.28
  31.6 1.3 copy.27
  32.9 1.0 copy.29
  33.9 2.2 %maximum_bitcast_fusion = bf16[16,2,128,128]{3,2,1,0:T(8,128)(2,1)} fusion(bf16[1,128,16,128]{3,1,0,2:T(8,128)(2,1)} %copy.29, bf16[1,128,16,128]{3,1,0,2:T(8,128)(2,1)S(1)} %copy.28), kind=kLoop, calls=%fused_computation.1 | loop fusion | flops 524288 | bytes 2097152 | tf_op jit(solution)/shard_map/transpose | solution.py:169
  36.1 4.0 %all-to-all-start = ((bf16[16,2,128,128]{3,2,1,0:T(8,128)(2,1)}), bf16[16,2,128,128]{3,2,1,0:T(8,128)(2,1)S(1)}, u32[]{:S(2)}, u32[]{:S(2)}) async-start(bf16[16,2,128,128]{3,2,1,0:T(8,128)(2,1)} %maximum_bitcast_fusion), calls=%async_computation | async-start | bytes 2097152 | tf_op jit(solution)/shard_map/all_to_all | solution.py:169
  40.4 13.5 %collective-permute-done.1.kv1_ref = bf16[16,2,128,128]{3,2,1,0:T(8,128)(2,1)S(1)} collective-permute-done((bf16[16,2,128,128]{3,2,1,0:T(8,128)(2,1)S(1)}, bf16[16,2,128,128]{3,2,1,0:T(8,128)(2,1)S(1)}, u32[]{:S(2)}, u32[]{:S(2)}) %collective-permute-start.1) | collective-permute-done | bytes 1048608 | tf_op jit(solution)/shard_map/ppermute | solution.py:163
  53.9 0.8 slice.32
  54.7 1.0 copy-done
  55.6 3.5 %collective-permute-start.2 = (bf16[7,2,128,128]{3,2,1,0:T(8,128)(2,1)}, bf16[7,2,128,128]{3,2,1,0:T(8,128)(2,1)S(1)}, u32[]{:S(2)}, u32[]{:S(2)}) collective-permute-start(bf16[7,2,128,128]{3,2,1,0:T(8,128)(2,1)} %slice.32), channel_id=1, source_target_pairs={{0,16},{16,32},{32,48},{48,64},{64,80},{80,96},{96,112},{112,128},... | collective-permute-start | bytes 1376264 | tf_op jit(solution)/shard_map/ppermute | solution.py:163
  59.2 0.4 and_reduce_fusion
  59.7 21.7 %collective-permute-done.2.kv2_ref = bf16[7,2,128,128]{3,2,1,0:T(8,128)(2,1)S(1)} collective-permute-done((bf16[7,2,128,128]{3,2,1,0:T(8,128)(2,1)}, bf16[7,2,128,128]{3,2,1,0:T(8,128)(2,1)S(1)}, u32[]{:S(2)}, u32[]{:S(2)}) %collective-permute-start.2) | collective-permute-done | bytes 458784 | tf_op jit(solution)/shard_map/ppermute | solution.py:163
  81.4 0.8 copy-done.2
  82.2 1.2 copy-done.1
  83.4 1.0 copy-done.3
  84.4 25.3 %attend.1 = (bf16[16,2,128,128]{3,2,1,0:T(8,128)(2,1)}, f32[16,2,128,128]{3,2,1,0:T(8,128)}, bf16[16,2,128,128]{3,2,1,0:T(8,128)(2,1)S(1)}, bf16[7,2,128,128]{3,2,1,0:T(8,128)(2,1)}) custom-call(s32[16,16]{1,0:T(8,128)S(1)} %get-tuple-element.25.tile_ref, s32[16,16]{1,0:T(8,128)S(1)} %get-tuple-element.24.start_ref, s32[8]{0:T(128)S(1)} %copy-done.4, ...), custom_call_target="tpu_custom_call" | custom-call | flops 6442450944 | bytes 12582912 | tf_op jit(solution)/shard_map/attend/pallas_call | solution.py:133
  109.7 5.2 %collective-permute-start.4 = (bf16[7,2,128,128]{3,2,1,0:T(8,128)(2,1)}, bf16[7,2,128,128]{3,2,1,0:T(8,128)(2,1)S(1)}, u32[]{:S(2)}, u32[]{:S(2)}) collective-permute-start(bf16[7,2,128,128]{3,2,1,0:T(8,128)(2,1)} %get-tuple-element.11), channel_id=1, source_target_pairs={{16,0},{32,16},{48,32},{64,48},{80,64},{96,80},{112,96},{128,112},... | collective-permute-start | bytes 1376264 | tf_op jit(solution)/shard_map/ppermute | solution.py:163
  114.9 5.4 %all-to-all-start.2 = ((bf16[16,2,128,128]{3,2,1,0:T(8,128)(2,1)}), bf16[16,2,128,128]{3,2,1,0:T(8,128)(2,1)S(1)}, u32[]{:S(2)}, u32[]{:S(2)}) async-start(bf16[16,2,128,128]{3,2,1,0:T(8,128)(2,1)} %get-tuple-element.8), calls=%async_computation.2 | async-start | bytes 2097152 | tf_op jit(solution)/shard_map/all_to_all | solution.py:173
  120.3 2.1 %collective-permute-start.3 = (bf16[9,2,128,128]{3,2,1,0:T(8,128)(2,1)S(1)}, bf16[9,2,128,128]{3,2,1,0:T(8,128)(2,1)S(1)}, u32[]{:S(2)}, u32[]{:S(2)}) collective-permute-start(bf16[9,2,128,128]{3,2,1,0:T(8,128)(2,1)S(1)} %slice.28), channel_id=1, source_target_pairs={{16,0},{32,16},{48,32},{64,48},{80,64},{96,80},{112,96},{128,112},... | collective-permute-start | bytes 1769480 | tf_op jit(solution)/shard_map/ppermute | solution.py:163
  122.4 0.9 collective-permute-done.4
  123.5 6.4 %collective-permute-start.5 = (bf16[7,2,128,128]{3,2,1,0:T(8,128)(2,1)S(1)}, bf16[7,2,128,128]{3,2,1,0:T(8,128)(2,1)S(1)}, u32[]{:S(2)}, u32[]{:S(2)}) collective-permute-start(bf16[7,2,128,128]{3,2,1,0:T(8,128)(2,1)S(1)} %add_convert_fusion.1), channel_id=1, source_target_pairs={{16,0},{32,16},{48,32},{64,48},{80,64},{96,80},{112,96},{128,112},... | collective-permute-start | bytes 1376264 | tf_op jit(solution)/shard_map/ppermute | solution.py:163
  129.9 7.2 %collective-permute-done.3 = bf16[9,2,128,128]{3,2,1,0:T(8,128)(2,1)S(1)} collective-permute-done((bf16[9,2,128,128]{3,2,1,0:T(8,128)(2,1)S(1)}, bf16[9,2,128,128]{3,2,1,0:T(8,128)(2,1)S(1)}, u32[]{:S(2)}, u32[]{:S(2)}) %collective-permute-start.3) | collective-permute-done | bytes 589856 | tf_op jit(solution)/shard_map/ppermute | solution.py:163
  137.1 9.8 %collective-permute-done.5 = bf16[7,2,128,128]{3,2,1,0:T(8,128)(2,1)S(1)} collective-permute-done((bf16[7,2,128,128]{3,2,1,0:T(8,128)(2,1)S(1)}, bf16[7,2,128,128]{3,2,1,0:T(8,128)(2,1)S(1)}, u32[]{:S(2)}, u32[]{:S(2)}) %collective-permute-start.5) | collective-permute-done | bytes 458784 | tf_op jit(solution)/shard_map/ppermute | solution.py:163
  147.0 1.3 add_convert_fusion
  148.3 7.8 %all-to-all-start.3 = ((bf16[16,2,128,128]{3,2,1,0:T(8,128)(2,1)}), bf16[16,2,128,128]{3,2,1,0:T(8,128)(2,1)S(1)}, u32[]{:S(2)}, u32[]{:S(2)}) async-start(bf16[16,2,128,128]{3,2,1,0:T(8,128)(2,1)} %add_convert_fusion), calls=%async_computation.3 | async-start | bytes 2097152 | tf_op jit(solution)/shard_map/all_to_all | solution.py:173
  156.5 1.0 copy.39
  157.8 1.0 copy.38
  158.8 15.0 %all-to-all-done.3 = bf16[16,2,128,128]{3,2,1,0:T(8,128)(2,1)S(1)} async-done(((bf16[16,2,128,128]{3,2,1,0:T(8,128)(2,1)}), bf16[16,2,128,128]{3,2,1,0:T(8,128)(2,1)S(1)}, u32[]{:S(2)}, u32[]{:S(2)}) %all-to-all-start.3) | async-done | bytes 1048608 | tf_op jit(solution)/shard_map/all_to_all | solution.py:173
  174.2 1.0 copy.41
  175.5 1.0 copy.40
  (35 shorter events, 3.1 us)
Async XLA Ops:
  0.6 1.7 copy-start.6
  3.0 28.0 %copy-start.7 = (bf16[128,2048]{1,0:T(8,128)(2,1)S(1)}, bf16[128,2048]{1,0:T(8,128)(2,1)}, u32[]{:S(2)}) copy-start(bf16[128,2048]{1,0:T(8,128)(2,1)} %param.6) | copy-start | bytes 1572868
  27.4 26.4 %collective-permute-start.1 = (bf16[16,2,128,128]{3,2,1,0:T(8,128)(2,1)S(1)}, bf16[16,2,128,128]{3,2,1,0:T(8,128)(2,1)S(1)}, u32[]{:S(2)}, u32[]{:S(2)}) collective-permute-start(bf16[16,2,128,128]{3,2,1,0:T(8,128)(2,1)S(1)} %all_to_all.20.kv0_ref), channel_id=1, source_target_pairs={{0,16},{16,32},{32,48},{48,64},{64,80},{80,96},{96,112},{112,128},... | collective-permute-start | bytes 3145736 | tf_op jit(solution)/shard_map/ppermute | solution.py:163
  33.9 6.2 %copy-start.8 = (s32[8,16]{1,0:T(8,128)S(1)}, s32[8,16]{1,0:T(8,128)}, u32[]{:S(2)}) copy-start(s32[8,16]{1,0:T(8,128)} %param.10) | copy-start | bytes 1540
  33.9 48.2 %copy-start.4 = (s32[8]{0:T(128)S(1)}, s32[8]{0:T(128)}, u32[]{:S(2)}) copy-start(s32[8]{0:T(128)} %doc_ref.1) | copy-start | bytes 100
  36.1 23.5 %all-to-all-start = ((bf16[16,2,128,128]{3,2,1,0:T(8,128)(2,1)}), bf16[16,2,128,128]{3,2,1,0:T(8,128)(2,1)S(1)}, u32[]{:S(2)}, u32[]{:S(2)}) async-start(bf16[16,2,128,128]{3,2,1,0:T(8,128)(2,1)} %maximum_bitcast_fusion), calls=%async_computation | async-start | bytes 2097152 | tf_op jit(solution)/shard_map/all_to_all | solution.py:169
  40.1 19.1 %collective-permute-start = (s32[8,16]{1,0:T(8,128)S(1)}, s32[8,16]{1,0:T(8,128)S(1)}, u32[]{:S(2)}, u32[]{:S(2)}) collective-permute-start(s32[8,16]{1,0:T(8,128)S(1)} %copy-done.8), channel_id=1, source_target_pairs={{0,8},{8,0},{1,9},{9,1},{2,10},{10,2},{3,11},{11,3},{4,12},{12,4},... | collective-permute-start | bytes 1544 | tf_op jit(solution)/shard_map/ppermute | solution.py:181
  54.7 1.0 copy-start
  55.6 25.8 %collective-permute-start.2 = (bf16[7,2,128,128]{3,2,1,0:T(8,128)(2,1)}, bf16[7,2,128,128]{3,2,1,0:T(8,128)(2,1)S(1)}, u32[]{:S(2)}, u32[]{:S(2)}) collective-permute-start(bf16[7,2,128,128]{3,2,1,0:T(8,128)(2,1)} %slice.32), channel_id=1, source_target_pairs={{0,16},{16,32},{32,48},{48,64},{64,80},{80,96},{96,112},{112,128},... | collective-permute-start | bytes 1376264 | tf_op jit(solution)/shard_map/ppermute | solution.py:163
  81.4 0.8 copy-start.2
  82.2 1.2 copy-start.1
  83.4 1.0 copy-start.3
  109.7 13.6 %collective-permute-start.4 = (bf16[7,2,128,128]{3,2,1,0:T(8,128)(2,1)}, bf16[7,2,128,128]{3,2,1,0:T(8,128)(2,1)S(1)}, u32[]{:S(2)}, u32[]{:S(2)}) collective-permute-start(bf16[7,2,128,128]{3,2,1,0:T(8,128)(2,1)} %get-tuple-element.11), channel_id=1, source_target_pairs={{16,0},{32,16},{48,32},{64,48},{80,64},{96,80},{112,96},{128,112},... | collective-permute-start | bytes 1376264 | tf_op jit(solution)/shard_map/ppermute | solution.py:163
  114.9 33.4 %all-to-all-start.2 = ((bf16[16,2,128,128]{3,2,1,0:T(8,128)(2,1)}), bf16[16,2,128,128]{3,2,1,0:T(8,128)(2,1)S(1)}, u32[]{:S(2)}, u32[]{:S(2)}) async-start(bf16[16,2,128,128]{3,2,1,0:T(8,128)(2,1)} %get-tuple-element.8), calls=%async_computation.2 | async-start | bytes 2097152 | tf_op jit(solution)/shard_map/all_to_all | solution.py:173
  120.3 26.7 %copy-start.5 = (f32[16,2,128,128]{3,2,1,0:T(8,128)S(1)}, f32[16,2,128,128]{3,2,1,0:T(8,128)}, u32[]{:S(2)}) copy-start(f32[16,2,128,128]{3,2,1,0:T(8,128)} %get-tuple-element.9) | copy-start | bytes 6291460
  120.3 16.8 %collective-permute-start.3 = (bf16[9,2,128,128]{3,2,1,0:T(8,128)(2,1)S(1)}, bf16[9,2,128,128]{3,2,1,0:T(8,128)(2,1)S(1)}, u32[]{:S(2)}, u32[]{:S(2)}) collective-permute-start(bf16[9,2,128,128]{3,2,1,0:T(8,128)(2,1)S(1)} %slice.28), channel_id=1, source_target_pairs={{16,0},{32,16},{48,32},{64,48},{80,64},{96,80},{112,96},{128,112},... | collective-permute-start | bytes 1769480 | tf_op jit(solution)/shard_map/ppermute | solution.py:163
  123.5 23.5 %collective-permute-start.5 = (bf16[7,2,128,128]{3,2,1,0:T(8,128)(2,1)S(1)}, bf16[7,2,128,128]{3,2,1,0:T(8,128)(2,1)S(1)}, u32[]{:S(2)}, u32[]{:S(2)}) collective-permute-start(bf16[7,2,128,128]{3,2,1,0:T(8,128)(2,1)S(1)} %add_convert_fusion.1), channel_id=1, source_target_pairs={{16,0},{32,16},{48,32},{64,48},{80,64},{96,80},{112,96},{128,112},... | collective-permute-start | bytes 1376264 | tf_op jit(solution)/shard_map/ppermute | solution.py:163
  148.3 25.6 %all-to-all-start.3 = ((bf16[16,2,128,128]{3,2,1,0:T(8,128)(2,1)}), bf16[16,2,128,128]{3,2,1,0:T(8,128)(2,1)S(1)}, u32[]{:S(2)}, u32[]{:S(2)}) async-start(bf16[16,2,128,128]{3,2,1,0:T(8,128)(2,1)} %add_convert_fusion), calls=%async_computation.3 | async-start | bytes 2097152 | tf_op jit(solution)/shard_map/all_to_all | solution.py:173

commit v2 on v1

v2 whole, which is shorter than its diff:
```python
import functools
import math

import jax
import jax.numpy as jnp
from jax import lax
from jax.experimental import pallas as pl
from jax.experimental.pallas import tpu as pltpu
from jax.sharding import Mesh
from jax.sharding import PartitionSpec as P

HD = 128
BLOCK = 128
KB = 16
WIN = 24
SCALE = HD**-0.5
EXPONENT = SCALE * math.log2(math.e)
GROUP = 4
CORES = ("core", "head")
NN = (((1,), (0,)), ((), ()))
NT = (((1,), (1,)), ((), ()))
TN = (((0,), (0,)), ((), ()))
SMEM = pl.BlockSpec(memory_space=pltpu.SMEM)
VMEM = pl.BlockSpec(memory_space=pltpu.VMEM)
ANYWHERE = pl.BlockSpec(memory_space=pltpu.HBM)


def dot(a, b, dims):
    return lax.dot_general(a, b, dims, preferred_element_type=jnp.float32)


def fold(x, op):
    return op(x.reshape(BLOCK // 8, 8, BLOCK), axis=0)


def rows_of(ref, tiles):
    return jnp.concatenate([ref[tile] for tile in tiles], axis=0)


def part(x, i):
    return x[i * BLOCK : (i + 1) * BLOCK]


def corners(pair):
    zero = jnp.zeros((BLOCK, HD), pair.dtype)
    top = jnp.concatenate([pair[:, :HD], zero], axis=1)
    return jnp.concatenate([top, jnp.concatenate([zero, pair[:, HD:]], axis=1)], axis=0)


def start_copies(pieces, target, sems, first):
    copies, at = [], 0
    for i, (ref, begin, count) in enumerate(pieces):
        copies.append(
            pltpu.make_async_copy(
                ref.at[pl.ds(begin, count)], target.at[pl.ds(at, count)], sems.at[first + i]
            )
        )
        at += count
    for copy in copies:
        copy.start()
    return copies


def doc_starts(doc_ref):
    starts, total = [], jnp.int32(0)
    for d in range(doc_ref.shape[0]):
        starts.append(total)
        total = total + doc_ref[d]
    return starts


def doc_begin(starts, query_pos):
    begin = jnp.zeros_like(query_pos)
    for start in starts:
        begin = jnp.where(start <= query_pos, start, begin)
    return begin


def blocks(count, kind):
    return jax.ShapeDtypeStruct((count, BLOCK, 2 * HD), kind)


def cost(tiles, matmuls):
    return pl.CostEstimate(
        flops=matmuls * tiles * BLOCK * BLOCK * HD // 4,
        bytes_accessed=1 << 20,
        transcendentals=0,
    )


def total_of(pieces):
    return sum(count for _, _, count in pieces)


def queries_kernel(unroll, first, count, shift_by, spans, done,
                   tile_ref, start_ref, doc_ref, qg_ref, *refs):
    kv_refs, refs = refs[: len(spans)], refs[len(spans) :]
    out_ref, stat_ref, kv, s_buf, d_buf, sems = refs[-6:]
    pieces = [(ref, *span) for ref, span in zip(kv_refs, spans)]
    copies = start_copies(pieces, kv, sems, 0)
    if done:
        rest = pl.ds(count, done)
        finished = [
            pltpu.make_async_copy(refs[0], out_ref.at[rest], sems.at[len(spans)]),
            pltpu.make_async_copy(refs[1], stat_ref.at[rest], sems.at[len(spans) + 1]),
        ]
        for copy in finished:
            copy.start()
    starts = doc_starts(doc_ref)
    sub = lax.broadcasted_iota(jnp.int32, (BLOCK, BLOCK), 0)
    lane = lax.broadcasted_iota(jnp.int32, (BLOCK, BLOCK), 1)
    lane_row = lax.broadcasted_iota(jnp.int32, (1, BLOCK), 1)
    for copy in copies:
        copy.wait()

    def one(t, slot):
        s_ref, d_ref = s_buf.at[slot], d_buf.at[slot]
        row = first + t
        qt, gt = qg_ref[row][:, :HD].T, qg_ref[row][:, HD:].T
        tiles = [tile_ref[row, i] - shift_by for i in range(KB)]
        begin = doc_begin(starts, start_ref[row, 0] + lane_row)
        peak = jnp.full((8, BLOCK), -3e38, jnp.float32)
        for j in range(0, KB, GROUP):
            scores = dot(rows_of(kv, tiles[j : j + GROUP])[:, :HD], qt, NN)
            for i in range(j, j + GROUP):
                allowed = sub >= begin - start_ref[row, i]
                if i == 0:
                    allowed = allowed & (sub <= lane)
                s = jnp.where(allowed, part(scores, i - j), -1e30)
                s_ref[i] = s
                peak = jnp.maximum(peak, fold(s, jnp.max))
        for j in range(0, KB, GROUP):
            d_rows = dot(rows_of(kv, tiles[j : j + GROUP])[:, HD:], gt, NN)
            d_ref[pl.ds(j, GROUP)] = d_rows.reshape(GROUP, BLOCK, BLOCK)
        peak = jnp.max(peak, axis=0, keepdims=True) * EXPONENT
        sum_p = jnp.zeros((8, BLOCK), jnp.float32)
        sum_d = jnp.zeros((8, BLOCK), jnp.float32)
        for i in range(KB):
            p = jnp.exp2(s_ref[i] * EXPONENT - peak)
            s_ref[i] = p
            sum_p = sum_p + fold(p, jnp.sum)
            sum_d = sum_d + fold(p * d_ref[i], jnp.sum)
        total = jnp.sum(sum_p, axis=0, keepdims=True)
        inv = 1.0 / total
        delta = jnp.sum(sum_d, axis=0, keepdims=True) * inv
        stat_ref[t, 0:1] = peak + jnp.log2(total)
        stat_ref[t, 1:2] = delta
        attended = jnp.zeros((BLOCK, HD), jnp.float32)
        grad_q = jnp.zeros((BLOCK, HD), jnp.float32)
        for j in range(0, KB, GROUP):
            group = range(j, j + GROUP)
            p = [s_ref[i] * inv for i in group]
            p_low = jnp.concatenate([x.astype(jnp.bfloat16) for x in p], axis=0)
            ds = jnp.concatenate(
                [(p[i - j] * (d_ref[i] - delta)).astype(jnp.bfloat16) for i in group], axis=0
            )
            kv_rows = rows_of(kv, tiles[j : j + GROUP])
            attended += dot(p_low, kv_rows[:, HD:], TN)
            grad_q += dot(ds, kv_rows[:, :HD], TN)
        out_ref[t, :, :HD] = attended.astype(jnp.bfloat16)
        out_ref[t, :, HD:] = (grad_q * SCALE).astype(jnp.bfloat16)

    def step(t, _):
        for u in range(unroll):
            one(t * unroll + u, u)
        return 0

    lax.fori_loop(0, count // unroll, step, 0)
    if done:
        for copy in finished:
            copy.wait()


def attend(tiles, starts, docs, qg, first, count, shift_by, pieces, done, after, unroll=4):
    spans = [piece[1:] for piece in pieces]
    done_rows = done[0].shape[0] if done else 0
    extra = [piece[0] for piece in pieces] + list(done) + list(after)
    return pl.pallas_call(
        functools.partial(queries_kernel, unroll, first, count, shift_by, spans, done_rows),
        out_shape=(
            blocks(count + done_rows, jnp.bfloat16),
            jax.ShapeDtypeStruct((count + done_rows, 2, BLOCK), jnp.float32),
        ),
        in_specs=[SMEM, SMEM, SMEM, VMEM] + [ANYWHERE] * len(extra),
        out_specs=(VMEM, VMEM),
        scratch_shapes=[
            pltpu.VMEM((total_of(pieces), BLOCK, 2 * HD), jnp.bfloat16),
            pltpu.VMEM((unroll, KB, BLOCK, BLOCK), jnp.float32),
            pltpu.VMEM((unroll, KB, BLOCK, BLOCK), jnp.float32),
            pltpu.SemaphoreType.DMA((len(pieces) + 2,)),
        ],
        compiler_params=pltpu.CompilerParams(vmem_limit_bytes=32 << 20),
        cost_estimate=cost(count * KB, 4),
        name="attend",
    )(tiles, starts, docs, qg, *extra)


def keys_kernel(
    unroll, rows, first, gap_at, gap, spans, n_qg, n_stat, carried,
    count_ref, tile_ref, doc_ref, base_ref, kv_ref, *refs,
):
    pieces = [(ref, *span) for ref, span in zip(refs, spans)]
    out_ref, qg, stat, acc, row_of, slot_of, sems = refs[-7:]
    copies = start_copies(pieces[:n_qg], qg, sems, 0)
    copies += start_copies(pieces[n_qg : n_qg + n_stat], stat, sems, n_qg)
    copies += start_copies(pieces[n_qg + n_stat :], acc, sems, n_qg + n_stat)
    if not carried:
        acc[...] = jnp.zeros_like(acc)
    starts = doc_starts(doc_ref)
    base = base_ref[0]
    sub = lax.broadcasted_iota(jnp.int32, (BLOCK, BLOCK), 0)
    lane_row = lax.broadcasted_iota(jnp.int32, (1, BLOCK), 1)

    def listed_row(r):
        return first + r + jnp.where(r >= gap_at, gap, 0)

    def list_row(r, at):
        def put(k, at):
            row_of[at] = r
            slot_of[at] = k * GROUP
            return at + 1

        groups = (count_ref[listed_row(r)] + (GROUP - 1)) >> (GROUP.bit_length() - 1)
        return lax.fori_loop(0, groups, put, at)

    items = lax.fori_loop(0, rows, list_row, jnp.int32(0))
    for u in range(unroll):
        row_of[items + u] = 0
        slot_of[items + u] = KB
    for copy in copies:
        copy.wait()

    def one(item):
        r, slot = row_of[item], slot_of[item]
        row = listed_row(r)
        count = count_ref[row]
        both = corners(qg[r])
        query_pos = base + row * BLOCK + lane_row
        begin = doc_begin(starts, query_pos)
        peak, delta = stat[r, 0:1], stat[r, 1:2]
        tiles = [tile_ref[row, slot + i] for i in range(GROUP)]
        scores = dot(rows_of(kv_ref, tiles), both, NT)
        weights = []
        for i in range(GROUP):
            start = jnp.where(slot + i < count, base + tiles[i] * BLOCK, 1 << 30)
            allowed = (sub >= begin - start) & (sub <= query_pos - start)
            s = part(scores, i)
            p = jnp.where(allowed, jnp.exp2(s[:, :BLOCK] * EXPONENT - peak), 0.0)
            ds = (p * (s[:, BLOCK:] - delta)).astype(jnp.bfloat16)
            weights.append(jnp.concatenate([ds, p.astype(jnp.bfloat16)], axis=1))
        return tiles, dot(jnp.concatenate(weights, axis=0), both, NN)

    def step(t, _):
        results = [one(t * unroll + u) for u in range(unroll)]
        for tiles, grads in results:
            for i in range(GROUP):
                acc[tiles[i]] += part(grads, i)
        return 0

    lax.fori_loop(0, lax.div(items + (unroll - 1), jnp.int32(unroll)), step, 0)
    if carried:
        out_ref[:, :, :HD] = (acc[:, :, :HD] * SCALE).astype(jnp.bfloat16)
        out_ref[:, :, HD:] = acc[:, :, HD:].astype(jnp.bfloat16)
    else:
        out_ref[...] = acc[...]


def key_grads(counts, tiles, docs, base, kv, first, gap_at, gap, qg, stat, carried, unroll=12):
    per, rows = kv.shape[0], total_of(qg)
    pieces = [*qg, *stat, *carried]
    spans = [piece[1:] for piece in pieces]
    items = rows * (KB // GROUP) + unroll
    return pl.pallas_call(
        functools.partial(
            keys_kernel, unroll, rows, first, gap_at, gap, spans, len(qg), len(stat), len(carried)
        ),
        out_shape=blocks(per, jnp.bfloat16 if carried else jnp.float32),
        in_specs=[SMEM, SMEM, SMEM, SMEM, VMEM] + [ANYWHERE] * len(pieces),
        out_specs=VMEM,
        scratch_shapes=[
            pltpu.VMEM((rows, BLOCK, 2 * HD), jnp.bfloat16),
            pltpu.VMEM((rows, 2, BLOCK), jnp.float32),
            pltpu.VMEM((per, BLOCK, 2 * HD), jnp.float32),
            pltpu.SMEM((items,), jnp.int32),
            pltpu.SMEM((items,), jnp.int32),
            pltpu.SemaphoreType.DMA((len(pieces),)),
        ],
        compiler_params=pltpu.CompilerParams(vmem_limit_bytes=32 << 20),
        cost_estimate=cost(rows * 8, 4),
        name="key_grads",
    )(counts, tiles, docs, base, kv, *[piece[0] for piece in pieces])


def run_copies(pairs, sems):
    copies = [
        pltpu.make_async_copy(source, target, sems.at[i])
        for i, (source, target) in enumerate(pairs)
    ]
    for copy in copies:
        copy.start()
    for copy in copies:
        copy.wait()


def columns(i):
    return pl.ds(i * HD, HD)


def pack_kernel(*refs):
    *ins, out_ref, sems = refs
    pairs = []
    for h in range(out_ref.shape[0]):
        for j, ref in enumerate(ins):
            pairs.append((ref.at[:, columns(h)], out_ref.at[h, j // 2, :, columns(j % 2)]))
    run_copies(pairs, sems)


def to_heads(*arrays):
    heads = arrays[0].shape[1] // HD
    packed = pl.pallas_call(
        pack_kernel,
        out_shape=jax.ShapeDtypeStruct((heads, len(arrays) // 2, BLOCK, 2 * HD), jnp.bfloat16),
        in_specs=[ANYWHERE] * len(arrays),
        out_specs=VMEM,
        scratch_shapes=[pltpu.SemaphoreType.DMA((heads * len(arrays),))],
        name="pack",
    )(*arrays)
    return lax.all_to_all(packed, CORES, 0, 0, tiled=True)


def unpack_kernel(pair_ref, a_ref, b_ref, sems):
    pairs = []
    for h in range(pair_ref.shape[0]):
        for j, ref in enumerate((a_ref, b_ref)):
            pairs.append((pair_ref.at[h, :, columns(j)], ref.at[:, columns(h)]))
    run_copies(pairs, sems)


def to_tokens(pair):
    pair = lax.all_to_all(pair, CORES, 0, 0, tiled=True)
    rows = jax.ShapeDtypeStruct((BLOCK, pair.shape[0] * HD), jnp.bfloat16)
    return pl.pallas_call(
        unpack_kernel,
        out_shape=(rows, rows),
        in_specs=[VMEM],
        out_specs=(VMEM, VMEM),
        scratch_shapes=[pltpu.SemaphoreType.DMA((2 * pair.shape[0],))],
        name="unpack",
    )(pair)


def shift(value, steps):
    count = lax.axis_size("yz")
    first, last = max(0, -steps), min(count, count - steps)
    return lax.ppermute(value, "yz", [(source, source + steps) for source in range(first, last)])


def on_device(queries, keys, values, grad_out, key_blocks, doc_lengths):
    per = lax.axis_size("core") * lax.axis_size("head")
    total = lax.axis_size("yz") * per
    far, half = WIN - 1 - per, per // 2
    first_block = lax.axis_index("yz") * per

    partner = lax.ppermute(key_blocks, "core", [(0, 1), (1, 0)])
    is_first = lax.axis_index("core") == 0
    listed = jnp.concatenate(
        [jnp.where(is_first, key_blocks, partner), jnp.where(is_first, partner, key_blocks)]
    )
    listed = jnp.concatenate([listed, shift(listed, -1), shift(listed[:far], -2)])
    everything = to_heads(keys, values, queries, grad_out)
    kv0, qg0 = everything[:, 0], everything[:, 1]
    kv1_high, qg1_low = shift(everything[per - far :, 0], 1), shift(everything[:far, 1], -1)
    kv1_low, qg1_high = shift(everything[: per - far, 0], 1), shift(everything[far:, 1], -1)
    kv2, qg2 = shift(kv1_high, 1), shift(qg1_low, -1)
    kv1 = [(kv1_low, 0, per - far), (kv1_high, 0, far)]
    qg1 = [(qg1_low, 0, far), (qg1_high, 0, per - far)]

    order = jnp.arange(KB)
    earlier = order[:, None] > order[None, :]
    repeated = jnp.any((listed[:, :, None] == listed[:, None, :]) & earlier, axis=2)
    tiles = listed[:per] - (first_block - (far + per))
    starts = jnp.where(repeated[:per], -(1 << 30), listed[:per] * BLOCK)
    local = listed - first_block
    real = first_block + jnp.arange(listed.shape[0]) < total
    wanted = (local >= 0) & (local < per) & jnp.logical_not(repeated) & real[:, None]
    rank = jnp.sum(jnp.where(wanted[:, None, :] & earlier, 1, 0), axis=2)
    taken = wanted[:, :, None] & (rank[:, :, None] == jnp.arange(KB + GROUP))
    own_tiles = jnp.sum(jnp.where(taken, local[:, :, None], 0), axis=1)
    counts = jnp.sum(wanted.astype(jnp.int32), axis=1)
    base = (first_block * BLOCK).reshape(1)

    late, late_stat = attend(
        tiles, starts, doc_lengths, qg0, half, half, far, [*kv1, (kv0, 0, per)], [], [qg1_low, qg1_high]
    )
    both, stat = attend(
        tiles, starts, doc_lengths, qg0, 0, half, 0,
        [(kv2, 0, far), *kv1, (kv0, 0, half)], [late, late_stat], [qg2],
    )
    sums = key_grads(
        counts, own_tiles, doc_lengths, base, kv0, 0, per, 0,
        [(qg0, 0, per)], [(stat, 0, per)], [],
    )
    attended, grad_q = to_tokens(both)
    grads = key_grads(
        counts, own_tiles, doc_lengths, base, kv0, per, per, 0,
        [*qg1, (qg2, 0, far)],
        [(shift(stat, -1), 0, per), (shift(stat, -2), 0, far)],
        [(sums, 0, per)],
    )
    grad_k, grad_v = to_tokens(grads)
    return attended, grad_q, grad_k, grad_v


def solution(mesh):
    blk, head = mesh.devices.shape
    grid = Mesh(mesh.devices.reshape(blk // 2, 2, head), ("yz", "core", "head"))
    rows = P(("yz", "core", "head"), None)
    return jax.shard_map(
        on_device,
        mesh=grid,
        in_specs=(rows, rows, rows, rows, P(("yz", "core"), None), P()),
        out_specs=(rows,) * 4,
        check_vma=False,
    )
```

time: 180 us -> 164 us (0.911); the launches traced: 177 us -> 162 us
  Pallas kernels: 25.3 us -> 51.8 us
  waiting for transfers between devices: 68.2 us -> 42 us
  blocking collectives: 24.4 us -> 0 us
  starting transfers between devices: 38.2 us -> 60.8 us
  local copies, waits for them, and re-layouts: 15.4 us -> 6.14 us
  other arithmetic: 4.18 us -> 0.53 us
    ppermute x5 -> x10, waiting for transfers between devices: 53.2 us -> 6.46 us  [shift(): lax.ppermute(value, 'yz', [(source, source + steps) for source in range(f...]
    pallas_call x1 -> x7, Pallas kernels: 25.3 us -> 51.8 us  [the longest x2 22.2 us: key_grads(): pl.pallas_call(functools.partial(keys_kernel, unroll, rows, first, gap_at...]
    all_to_all x1 -> x0, blocking collectives: 24.4 us -> none  [to_heads(): return lax.all_to_all(pair.transpose(2, 0, 1, 3), CORES, 0, 0, tiled=True)]
    ppermute x5 -> x10, starting transfers between devices: 20.7 us -> 41 us  [shift(): lax.ppermute(value, 'yz', [(source, source + steps) for source in range(f...]
    all_to_all x1, waiting for transfers between devices: 0.01 us -> 19.6 us  [to_heads(): return lax.all_to_all(packed, CORES, 0, 0, tiled=True)]
    unnamed x26 -> x14, local copies, waits for them, and re-layouts: 11.3 us -> 1.99 us
    squeeze x0 -> x3, local copies, waits for them, and re-layouts: none -> 3.71 us  [the longest x1 1.69 us: on_device(): kv0, qg0 = (everything[:, 0], everything[:, 1])]
    all_to_all x1, starting transfers between devices: 3.98 us -> 6.73 us  [to_heads(): return lax.all_to_all(packed, CORES, 0, 0, tiled=True)]
  transfers between devices with their start and end apart: 9 -> 14, of which waited for: 6 -> 6; matrix products, arithmetic and copies ran while one was open for 6% -> 3% of each run, Pallas kernels for 0% -> 22%
where the time goes in v2:
time: 164 us; the launch traced here: 162 us
  starting transfers between devices  60.8 us (37%)
  Pallas kernels  51.8 us (32%)
  waiting for transfers between devices  42 us (26%)
  local copies, waits for them, and re-layouts  6.14 us (4%)
    ppermute x10, starting transfers between devices, shift(): lax.ppermute(value, 'yz', [(source, source + steps) for source in range(f...  41 us
    pallas_call x2, Pallas kernels, key_grads(): pl.pallas_call(functools.partial(keys_kernel, unroll, rows, first, gap_at...  22.2 us
    pallas_call x2, Pallas kernels, attend(): pl.pallas_call(functools.partial(queries_kernel, unroll, first, count, sh...  20.5 us
    all_to_all x1, waiting for transfers between devices, to_heads(): return lax.all_to_all(packed, CORES, 0, 0, tiled=True)  19.6 us
    all_to_all x2, waiting for transfers between devices, to_tokens(): pair = lax.all_to_all(pair, CORES, 0, 0, tiled=True)  14.9 us
    all_to_all x2, starting transfers between devices, to_tokens(): pair = lax.all_to_all(pair, CORES, 0, 0, tiled=True)  12.9 us
    all_to_all x1, starting transfers between devices, to_heads(): return lax.all_to_all(packed, CORES, 0, 0, tiled=True)  6.73 us
    ppermute x10, waiting for transfers between devices, shift(): lax.ppermute(value, 'yz', [(source, source + steps) for source in range(f...  6.46 us
  transfers between devices with their start and end apart: 14, of which 6 were waited for; matrix products, arithmetic and copies ran while one was open for 3% of the time, Pallas kernels for 22%

profile of v2, /device:TPU:41, one launch (start us, length us, event | category | flops | bytes accessed | tf_op | source)
XLA Modules:
  0.0 162.4 jit_solution(12326147256912715449)
XLA Ops:
  0.6 3.4 %pack.1 = bf16[16,2,128,256]{3,2,1,0:T(8,128)(2,1)} custom-call(bf16[128,2048]{1,0:T(8,128)(2,1)} %refs_0_.1, bf16[128,2048]{1,0:T(8,128)(2,1)} %refs_1_.1, bf16[128,2048]{1,0:T(8,128)(2,1)} %refs_2_.1, bf16[128,2048]{1,0:T(8,128)(2,1)} %refs_3_.1), custom_call_target="tpu_custom_call" | custom-call | tf_op jit(solution)/shard_map/pack/pallas_call | solution.py:320
  4.1 6.7 %all-to-all-start = ((bf16[16,2,128,256]{3,2,1,0:T(8,128)(2,1)}), bf16[16,2,128,256]{3,2,1,0:T(8,128)(2,1)S(1)}, u32[]{:S(2)}, u32[]{:S(2)}) async-start(bf16[16,2,128,256]{3,2,1,0:T(8,128)(2,1)} %pack.1), calls=%async_computation | async-start | bytes 4194304 | tf_op jit(solution)/shard_map/all_to_all | solution.py:328
  10.8 0.2 collective-permute-start
  11.0 1.1 collective-permute-done
  12.1 1.9 %collective-permute-start.1 = (s32[16,16]{1,0:T(8,128)S(1)}, s32[16,16]{1,0:T(8,128)S(1)}, u32[]{:S(2)}, u32[]{:S(2)}) collective-permute-start(s32[16,16]{1,0:T(8,128)S(1)} %pad_add_fusion.1), channel_id=1, source_target_pairs={{16,0},{32,16},{48,32},{64,48},{80,64},{96,80},{112,96},{128,112},... | collective-permute-start | bytes 3080 | tf_op jit(solution)/shard_map/ppermute | solution.py:355
  14.0 8.5 %collective-permute-start.2 = (s32[7,16]{1,0:T(8,128)S(1)}, s32[7,16]{1,0:T(8,128)S(1)}, u32[]{:S(2)}, u32[]{:S(2)}) collective-permute-start(s32[7,16]{1,0:T(8,128)S(1)} %bitcast.26), channel_id=1, source_target_pairs={{32,0},{48,16},{64,32},{80,48},{96,64},{112,80},{128,96},{144,112}... | collective-permute-start | bytes 1352 | tf_op jit(solution)/shard_map/ppermute | solution.py:355
  22.6 19.6 %all-to-all-done = bf16[16,2,128,256]{3,2,1,0:T(8,128)(2,1)S(1)} async-done(((bf16[16,2,128,256]{3,2,1,0:T(8,128)(2,1)}), bf16[16,2,128,256]{3,2,1,0:T(8,128)(2,1)S(1)}, u32[]{:S(2)}, u32[]{:S(2)}) %all-to-all-start) | async-done | bytes 2097184 | tf_op jit(solution)/shard_map/all_to_all | solution.py:328
  42.2 0.9 slice_bitcast_fusion.4
  43.1 3.5 %collective-permute-start.3 = (bf16[7,128,256]{2,1,0:T(8,128)(2,1)S(1)}, bf16[7,128,256]{2,1,0:T(8,128)(2,1)}, u32[]{:S(2)}, u32[]{:S(2)}) collective-permute-start(bf16[7,128,256]{2,1,0:T(8,128)(2,1)S(1)} %get-tuple-element.26), channel_id=1, source_target_pairs={{0,16},{16,32},{32,48},{48,64},{64,80},{80,96},{96,112},{112,128},... | collective-permute-start | bytes 1376264 | tf_op jit(solution)/shard_map/ppermute | solution.py:355
  46.7 1.9 %collective-permute-start.6 = (bf16[7,128,256]{2,1,0:T(8,128)(2,1)}, bf16[7,128,256]{2,1,0:T(8,128)(2,1)}, u32[]{:S(2)}, u32[]{:S(2)}) collective-permute-start(bf16[7,128,256]{2,1,0:T(8,128)(2,1)} %get-tuple-element.25), channel_id=1, source_target_pairs={{16,0},{32,16},{48,32},{64,48},{80,64},{96,80},{112,96},{128,112},... | collective-permute-start | bytes 1376264 | tf_op jit(solution)/shard_map/ppermute | solution.py:355
  48.7 1.1 slice_bitcast_fusion.2
  49.8 3.5 %collective-permute-start.5 = (bf16[9,128,256]{2,1,0:T(8,128)(2,1)}, bf16[9,128,256]{2,1,0:T(8,128)(2,1)S(1)}, u32[]{:S(2)}, u32[]{:S(2)}) collective-permute-start(bf16[9,128,256]{2,1,0:T(8,128)(2,1)} %get-tuple-element.24), channel_id=1, source_target_pairs={{0,16},{16,32},{32,48},{48,64},{64,80},{80,96},{96,112},{112,128},... | collective-permute-start | bytes 1769480 | tf_op jit(solution)/shard_map/ppermute | solution.py:355
  53.3 4.8 %collective-permute-start.7 = (bf16[9,128,256]{2,1,0:T(8,128)(2,1)}, bf16[9,128,256]{2,1,0:T(8,128)(2,1)S(1)}, u32[]{:S(2)}, u32[]{:S(2)}) collective-permute-start(bf16[9,128,256]{2,1,0:T(8,128)(2,1)} %get-tuple-element.23), channel_id=1, source_target_pairs={{16,0},{32,16},{48,32},{64,48},{80,64},{96,80},{112,96},{128,112},... | collective-permute-start | bytes 1769480 | tf_op jit(solution)/shard_map/ppermute | solution.py:355
  58.4 2.4 %collective-permute-done.6.refs_3_.refs_0_ = bf16[7,128,256]{2,1,0:T(8,128)(2,1)} collective-permute-done((bf16[7,128,256]{2,1,0:T(8,128)(2,1)}, bf16[7,128,256]{2,1,0:T(8,128)(2,1)}, u32[]{:S(2)}, u32[]{:S(2)}) %collective-permute-start.6) | collective-permute-done | bytes 458784 | tf_op jit(solution)/shard_map/ppermute | solution.py:355
  60.9 4.2 %collective-permute-start.8 = (bf16[7,128,256]{2,1,0:T(8,128)(2,1)}, bf16[7,128,256]{2,1,0:T(8,128)(2,1)S(1)}, u32[]{:S(2)}, u32[]{:S(2)}) collective-permute-start(bf16[7,128,256]{2,1,0:T(8,128)(2,1)} %collective-permute-done.6.refs_3_.refs_0_), channel_id=1, source_target_pairs={{16,0},{32,16},{48,32},{64,48},{80,64},{96,80},{112,96},{128,112},... | collective-permute-start | bytes 1376264 | tf_op jit(solution)/shard_map/ppermute | solution.py:355
  65.1 2.6 %collective-permute-start.4 = (bf16[7,128,256]{2,1,0:T(8,128)(2,1)}, bf16[7,128,256]{2,1,0:T(8,128)(2,1)S(1)}, u32[]{:S(2)}, u32[]{:S(2)}) collective-permute-start(bf16[7,128,256]{2,1,0:T(8,128)(2,1)} %collective-permute-done.3.refs_1_.refs_2_), channel_id=1, source_target_pairs={{0,16},{16,32},{32,48},{48,64},{64,80},{80,96},{96,112},{112,128},... | collective-permute-start | bytes 1376264 | tf_op jit(solution)/shard_map/ppermute | solution.py:355
  67.7 1.7 %slice_bitcast_fusion = (bf16[16,128,256]{2,1,0:T(8,128)(2,1)S(1)}, bf16[16,128,256]{2,1,0:T(8,128)(2,1)S(1)}) fusion(bf16[16,2,128,256]{3,2,1,0:T(8,128)(2,1)} %copy-done.4), kind=kLoop, calls=%fused_computation | loop fusion | bytes 4194304 | tf_op jit(solution)/shard_map/squeeze | solution.py:371
  69.4 0.3 collective-permute-done.5.refs_0_.refs_1_
  69.7 3.7 %collective-permute-done.7.refs_4_.refs_1_ = bf16[9,128,256]{2,1,0:T(8,128)(2,1)S(1)} collective-permute-done((bf16[9,128,256]{2,1,0:T(8,128)(2,1)}, bf16[9,128,256]{2,1,0:T(8,128)(2,1)S(1)}, u32[]{:S(2)}, u32[]{:S(2)}) %collective-permute-start.7) | collective-permute-done | bytes 589856 | tf_op jit(solution)/shard_map/ppermute | solution.py:355
  73.4 10.1 %attend.2 = (bf16[8,128,256]{2,1,0:T(8,128)(2,1)S(1)}, f32[8,2,128]{2,1,0:T(2,128)S(1)}) custom-call(s32[16,16]{1,0:T(8,128)S(1)} %get-tuple-element.30.tile_ref, s32[16,16]{1,0:T(8,128)S(1)} %get-tuple-element.29.start_ref, s32[8]{0:T(128)S(1)} %copy-done.3, bf16[16,128,256]{2,1,0:T(8,128)(2,1)S(1)} %get-tuple-element.28.qg_ref.refs_0_, ...), custom_call_target="tpu_custom_call" | custom-call | flops 268435456 | bytes 1048576 | tf_op jit(solution)/shard_map/attend/pallas_call | solution.py:178
  83.6 10.4 %attend.3 = (bf16[16,128,256]{2,1,0:T(8,128)(2,1)S(1)}, f32[16,2,128]{2,1,0:T(2,128)S(1)}) custom-call(s32[16,16]{1,0:T(8,128)S(1)} %get-tuple-element.30.tile_ref, s32[16,16]{1,0:T(8,128)S(1)} %get-tuple-element.29.start_ref, s32[8]{0:T(128)S(1)} %copy-done.3, bf16[16,128,256]{2,1,0:T(8,128)(2,1)S(1)} %get-tuple-element.28.qg_ref.refs_0_, ...), custom_call_target="tpu_custom_call" | custom-call | flops 268435456 | bytes 1048576 | tf_op jit(solution)/shard_map/attend/pallas_call | solution.py:178
  94.0 1.0 copy-done.2
  95.0 6.0 %all-to-all-start.1 = ((bf16[16,128,256]{2,1,0:T(8,128)(2,1)}), bf16[16,128,256]{2,1,0:T(8,128)(2,1)}, u32[]{:S(2)}, u32[]{:S(2)}) async-start(bf16[16,128,256]{2,1,0:T(8,128)(2,1)} %copy-done.2), calls=%async_computation.1 | async-start | bytes 2097152 | tf_op jit(solution)/shard_map/all_to_all | solution.py:340
  101.6 8.0 %collective-permute-start.10 = (f32[16,2,128]{2,1,0:T(2,128)S(1)}, f32[16,2,128]{2,1,0:T(2,128)S(1)}, u32[]{:S(2)}, u32[]{:S(2)}) collective-permute-start(f32[16,2,128]{2,1,0:T(2,128)S(1)} %get-tuple-element.17.refs_1_), channel_id=1, source_target_pairs={{32,0},{48,16},{64,32},{80,48},{96,64},{112,80},{128,96},{144,112}... | collective-permute-start | bytes 49160 | tf_op jit(solution)/shard_map/ppermute | solution.py:355
  109.6 1.9 %collective-permute-start.9 = (f32[16,2,128]{2,1,0:T(2,128)S(1)}, f32[16,2,128]{2,1,0:T(2,128)S(1)}, u32[]{:S(2)}, u32[]{:S(2)}) collective-permute-start(f32[16,2,128]{2,1,0:T(2,128)S(1)} %get-tuple-element.17.refs_1_), channel_id=1, source_target_pairs={{16,0},{32,16},{48,32},{64,48},{80,64},{96,80},{112,96},{128,112},... | collective-permute-start | bytes 49160 | tf_op jit(solution)/shard_map/ppermute | solution.py:355
  111.5 8.1 %key_grads.2.refs_5_ = f32[16,128,256]{2,1,0:T(8,128)S(1)} custom-call(s32[39]{0:T(128)S(1)} %get-tuple-element.20.count_ref, s32[39,20]{1,0:T(8,128)S(1)} %copy.54.tile_ref, s32[8]{0:T(128)S(1)} %copy-done.3, s32[1]{0:T(128)} %bitcast.6.base_ref, bf16[16,128,256]{2,1,0:T(8,128)(2,1)S(1)} %get-tuple-element.27.refs_2_.refs_3_.kv_ref, ...), custom_call_target="tpu_custom_call" | custom-call | flops 268435456 | bytes 1048576 | tf_op jit(solution)/shard_map/key_grads/pallas_call | solution.py:273
  119.7 14.1 %key_grads.3 = bf16[16,128,256]{2,1,0:T(8,128)(2,1)} custom-call(s32[39]{0:T(128)S(1)} %get-tuple-element.20.count_ref, s32[39,20]{1,0:T(8,128)S(1)} %copy.54.tile_ref, s32[8]{0:T(128)S(1)} %copy-done.3, s32[1]{0:T(128)} %bitcast.6.base_ref, bf16[16,128,256]{2,1,0:T(8,128)(2,1)S(1)} %get-tuple-element.27.refs_2_.refs_3_.kv_ref, ...), custom_call_target="tpu_custom_call" | custom-call | flops 385875968 | bytes 1048576 | tf_op jit(solution)/shard_map/key_grads/pallas_call | solution.py:273
  133.8 6.9 %all-to-all-start.2 = ((bf16[16,128,256]{2,1,0:T(8,128)(2,1)}), bf16[16,128,256]{2,1,0:T(8,128)(2,1)S(1)}, u32[]{:S(2)}, u32[]{:S(2)}) async-start(bf16[16,128,256]{2,1,0:T(8,128)(2,1)} %key_grads.3), calls=%async_computation.2 | async-start | bytes 2097152 | tf_op jit(solution)/shard_map/all_to_all | solution.py:340
  140.7 2.8 %unpack.2 = (bf16[128,2048]{1,0:T(8,128)(2,1)}, bf16[128,2048]{1,0:T(8,128)(2,1)}) custom-call(bf16[16,128,256]{2,1,0:T(8,128)(2,1)} %all-to-all-done.1.pair_ref), custom_call_target="tpu_custom_call" | custom-call | tf_op jit(solution)/shard_map/unpack/pallas_call | solution.py:342
  143.5 14.9 %all-to-all-done.2.pair_ref = bf16[16,128,256]{2,1,0:T(8,128)(2,1)S(1)} async-done(((bf16[16,128,256]{2,1,0:T(8,128)(2,1)}), bf16[16,128,256]{2,1,0:T(8,128)(2,1)S(1)}, u32[]{:S(2)}, u32[]{:S(2)}) %all-to-all-start.2) | async-done | bytes 1048608 | tf_op jit(solution)/shard_map/all_to_all | solution.py:340
  158.4 1.0 copy-done.5
  159.4 2.8 %unpack.3 = (bf16[128,2048]{1,0:T(8,128)(2,1)}, bf16[128,2048]{1,0:T(8,128)(2,1)}) custom-call(bf16[16,128,256]{2,1,0:T(8,128)(2,1)} %copy-done.5), custom_call_target="tpu_custom_call" | custom-call | tf_op jit(solution)/shard_map/unpack/pallas_call | solution.py:342
  (35 shorter events, 1.0 us)
Async XLA Ops:
  4.1 6.7 %copy-start.6 = (s32[8,16]{1,0:T(8,128)S(1)}, s32[8,16]{1,0:T(8,128)}, u32[]{:S(2)}) copy-start(s32[8,16]{1,0:T(8,128)} %param.10) | copy-start | bytes 1540
  4.1 38.1 %all-to-all-start = ((bf16[16,2,128,256]{3,2,1,0:T(8,128)(2,1)}), bf16[16,2,128,256]{3,2,1,0:T(8,128)(2,1)S(1)}, u32[]{:S(2)}, u32[]{:S(2)}) async-start(bf16[16,2,128,256]{3,2,1,0:T(8,128)(2,1)} %pack.1), calls=%async_computation | async-start | bytes 4194304 | tf_op jit(solution)/shard_map/all_to_all | solution.py:328
  10.8 1.3 collective-permute-start
  12.1 36.5 %collective-permute-start.1 = (s32[16,16]{1,0:T(8,128)S(1)}, s32[16,16]{1,0:T(8,128)S(1)}, u32[]{:S(2)}, u32[]{:S(2)}) collective-permute-start(s32[16,16]{1,0:T(8,128)S(1)} %pad_add_fusion.1), channel_id=1, source_target_pairs={{16,0},{32,16},{48,32},{64,48},{80,64},{96,80},{112,96},{128,112},... | collective-permute-start | bytes 3080 | tf_op jit(solution)/shard_map/ppermute | solution.py:355
  14.0 34.6 %collective-permute-start.2 = (s32[7,16]{1,0:T(8,128)S(1)}, s32[7,16]{1,0:T(8,128)S(1)}, u32[]{:S(2)}, u32[]{:S(2)}) collective-permute-start(s32[7,16]{1,0:T(8,128)S(1)} %bitcast.26), channel_id=1, source_target_pairs={{32,0},{48,16},{64,32},{80,48},{96,64},{112,80},{128,96},{144,112}... | collective-permute-start | bytes 1352 | tf_op jit(solution)/shard_map/ppermute | solution.py:355
  42.2 7.6 %copy-start.4 = (bf16[16,2,128,256]{3,2,1,0:T(8,128)(2,1)}, bf16[16,2,128,256]{3,2,1,0:T(8,128)(2,1)S(1)}, u32[]{:S(2)}) copy-start(bf16[16,2,128,256]{3,2,1,0:T(8,128)(2,1)S(1)} %all-to-all-done) | copy-start | bytes 6291460
  43.1 21.9 %collective-permute-start.3 = (bf16[7,128,256]{2,1,0:T(8,128)(2,1)S(1)}, bf16[7,128,256]{2,1,0:T(8,128)(2,1)}, u32[]{:S(2)}, u32[]{:S(2)}) collective-permute-start(bf16[7,128,256]{2,1,0:T(8,128)(2,1)S(1)} %get-tuple-element.26), channel_id=1, source_target_pairs={{0,16},{16,32},{32,48},{48,64},{64,80},{80,96},{96,112},{112,128},... | collective-permute-start | bytes 1376264 | tf_op jit(solution)/shard_map/ppermute | solution.py:355
  46.7 14.2 %collective-permute-start.6 = (bf16[7,128,256]{2,1,0:T(8,128)(2,1)}, bf16[7,128,256]{2,1,0:T(8,128)(2,1)}, u32[]{:S(2)}, u32[]{:S(2)}) collective-permute-start(bf16[7,128,256]{2,1,0:T(8,128)(2,1)} %get-tuple-element.25), channel_id=1, source_target_pairs={{16,0},{32,16},{48,32},{64,48},{80,64},{96,80},{112,96},{128,112},... | collective-permute-start | bytes 1376264 | tf_op jit(solution)/shard_map/ppermute | solution.py:355
  49.8 19.9 %collective-permute-start.5 = (bf16[9,128,256]{2,1,0:T(8,128)(2,1)}, bf16[9,128,256]{2,1,0:T(8,128)(2,1)S(1)}, u32[]{:S(2)}, u32[]{:S(2)}) collective-permute-start(bf16[9,128,256]{2,1,0:T(8,128)(2,1)} %get-tuple-element.24), channel_id=1, source_target_pairs={{0,16},{16,32},{32,48},{48,64},{64,80},{80,96},{96,112},{112,128},... | collective-permute-start | bytes 1769480 | tf_op jit(solution)/shard_map/ppermute | solution.py:355
  53.3 20.0 %collective-permute-start.7 = (bf16[9,128,256]{2,1,0:T(8,128)(2,1)}, bf16[9,128,256]{2,1,0:T(8,128)(2,1)S(1)}, u32[]{:S(2)}, u32[]{:S(2)}) collective-permute-start(bf16[9,128,256]{2,1,0:T(8,128)(2,1)} %get-tuple-element.23), channel_id=1, source_target_pairs={{16,0},{32,16},{48,32},{64,48},{80,64},{96,80},{112,96},{128,112},... | collective-permute-start | bytes 1769480 | tf_op jit(solution)/shard_map/ppermute | solution.py:355
  60.9 22.7 %collective-permute-start.8 = (bf16[7,128,256]{2,1,0:T(8,128)(2,1)}, bf16[7,128,256]{2,1,0:T(8,128)(2,1)S(1)}, u32[]{:S(2)}, u32[]{:S(2)}) collective-permute-start(bf16[7,128,256]{2,1,0:T(8,128)(2,1)} %collective-permute-done.6.refs_3_.refs_0_), channel_id=1, source_target_pairs={{16,0},{32,16},{48,32},{64,48},{80,64},{96,80},{112,96},{128,112},... | collective-permute-start | bytes 1376264 | tf_op jit(solution)/shard_map/ppermute | solution.py:355
  65.1 18.5 %collective-permute-start.4 = (bf16[7,128,256]{2,1,0:T(8,128)(2,1)}, bf16[7,128,256]{2,1,0:T(8,128)(2,1)S(1)}, u32[]{:S(2)}, u32[]{:S(2)}) collective-permute-start(bf16[7,128,256]{2,1,0:T(8,128)(2,1)} %collective-permute-done.3.refs_1_.refs_2_), channel_id=1, source_target_pairs={{0,16},{16,32},{32,48},{48,64},{64,80},{80,96},{96,112},{112,128},... | collective-permute-start | bytes 1376264 | tf_op jit(solution)/shard_map/ppermute | solution.py:355
  67.7 5.7 %copy-start.3 = (s32[8]{0:T(128)S(1)}, s32[8]{0:T(128)}, u32[]{:S(2)}) copy-start(s32[8]{0:T(128)} %doc_ref.7) | copy-start | bytes 100
  83.5 10.4 %copy-start = (bf16[7,128,256]{2,1,0:T(8,128)(2,1)}, bf16[7,128,256]{2,1,0:T(8,128)(2,1)S(1)}, u32[]{:S(2)}) copy-start(bf16[7,128,256]{2,1,0:T(8,128)(2,1)S(1)} %collective-permute-done.8.refs_6_.refs_2_) | copy-start | bytes 1376260
  94.0 1.0 copy-start.2
  95.0 38.8 %all-to-all-start.1 = ((bf16[16,128,256]{2,1,0:T(8,128)(2,1)}), bf16[16,128,256]{2,1,0:T(8,128)(2,1)}, u32[]{:S(2)}, u32[]{:S(2)}) async-start(bf16[16,128,256]{2,1,0:T(8,128)(2,1)} %copy-done.2), calls=%async_computation.1 | async-start | bytes 2097152 | tf_op jit(solution)/shard_map/all_to_all | solution.py:340
  101.6 18.0 %collective-permute-start.10 = (f32[16,2,128]{2,1,0:T(2,128)S(1)}, f32[16,2,128]{2,1,0:T(2,128)S(1)}, u32[]{:S(2)}, u32[]{:S(2)}) collective-permute-start(f32[16,2,128]{2,1,0:T(2,128)S(1)} %get-tuple-element.17.refs_1_), channel_id=1, source_target_pairs={{32,0},{48,16},{64,32},{80,48},{96,64},{112,80},{128,96},{144,112}... | collective-permute-start | bytes 49160 | tf_op jit(solution)/shard_map/ppermute | solution.py:355
  109.6 10.0 %collective-permute-start.9 = (f32[16,2,128]{2,1,0:T(2,128)S(1)}, f32[16,2,128]{2,1,0:T(2,128)S(1)}, u32[]{:S(2)}, u32[]{:S(2)}) collective-permute-start(f32[16,2,128]{2,1,0:T(2,128)S(1)} %get-tuple-element.17.refs_1_), channel_id=1, source_target_pairs={{16,0},{32,16},{48,32},{64,48},{80,64},{96,80},{112,96},{128,112},... | collective-permute-start | bytes 49160 | tf_op jit(solution)/shard_map/ppermute | solution.py:355
  111.5 8.1 %copy-start.1 = (bf16[7,128,256]{2,1,0:T(8,128)(2,1)S(1)}, bf16[7,128,256]{2,1,0:T(8,128)(2,1)}, u32[]{:S(2)}) copy-start(bf16[7,128,256]{2,1,0:T(8,128)(2,1)} %copy-done) | copy-start | bytes 1376260
  133.8 24.6 %all-to-all-start.2 = ((bf16[16,128,256]{2,1,0:T(8,128)(2,1)}), bf16[16,128,256]{2,1,0:T(8,128)(2,1)S(1)}, u32[]{:S(2)}, u32[]{:S(2)}) async-start(bf16[16,128,256]{2,1,0:T(8,128)(2,1)} %key_grads.3), calls=%async_computation.2 | async-start | bytes 2097152 | tf_op jit(solution)/shard_map/all_to_all | solution.py:340
  158.4 1.0 copy-start.5

commit v3 on v2

--- a/solution.py
+++ b/solution.py
@@ -196,23 +196,18 @@
 
 
 def keys_kernel(
-    unroll, rows, first, gap_at, gap, spans, n_qg, n_stat, carried,
+    unroll, rows, spans, n_qg,
     count_ref, tile_ref, doc_ref, base_ref, kv_ref, *refs,
 ):
     pieces = [(ref, *span) for ref, span in zip(refs, spans)]
     out_ref, qg, stat, acc, row_of, slot_of, sems = refs[-7:]
     copies = start_copies(pieces[:n_qg], qg, sems, 0)
-    copies += start_copies(pieces[n_qg : n_qg + n_stat], stat, sems, n_qg)
-    copies += start_copies(pieces[n_qg + n_stat :], acc, sems, n_qg + n_stat)
-    if not carried:
-        acc[...] = jnp.zeros_like(acc)
+    copies += start_copies(pieces[n_qg:], stat, sems, n_qg)
+    acc[...] = jnp.zeros_like(acc)
     starts = doc_starts(doc_ref)
     base = base_ref[0]
     sub = lax.broadcasted_iota(jnp.int32, (BLOCK, BLOCK), 0)
     lane_row = lax.broadcasted_iota(jnp.int32, (1, BLOCK), 1)
-
-    def listed_row(r):
-        return first + r + jnp.where(r >= gap_at, gap, 0)
 
     def list_row(r, at):
         def put(k, at):
@@ -220,7 +215,7 @@
             slot_of[at] = k * GROUP
             return at + 1
 
-        groups = (count_ref[listed_row(r)] + (GROUP - 1)) >> (GROUP.bit_length() - 1)
+        groups = (count_ref[r] + (GROUP - 1)) >> (GROUP.bit_length() - 1)
         return lax.fori_loop(0, groups, put, at)
 
     items = lax.fori_loop(0, rows, list_row, jnp.int32(0))
@@ -232,13 +227,12 @@
 
     def one(item):
         r, slot = row_of[item], slot_of[item]
-        row = listed_row(r)
-        count = count_ref[row]
+        count = count_ref[r]
         both = corners(qg[r])
-        query_pos = base + row * BLOCK + lane_row
+        query_pos = base + r * BLOCK + lane_row
         begin = doc_begin(starts, query_pos)
         peak, delta = stat[r, 0:1], stat[r, 1:2]
-        tiles = [tile_ref[row, slot + i] for i in range(GROUP)]
+        tiles = [tile_ref[r, slot + i] for i in range(GROUP)]
         scores = dot(rows_of(kv_ref, tiles), both, NT)
         weights = []
         for i in range(GROUP):
@@ -258,23 +252,18 @@
         return 0
 
     lax.fori_loop(0, lax.div(items + (unroll - 1), jnp.int32(unroll)), step, 0)
-    if carried:
-        out_ref[:, :, :HD] = (acc[:, :, :HD] * SCALE).astype(jnp.bfloat16)
-        out_ref[:, :, HD:] = acc[:, :, HD:].astype(jnp.bfloat16)
-    else:
-        out_ref[...] = acc[...]
-
-
-def key_grads(counts, tiles, docs, base, kv, first, gap_at, gap, qg, stat, carried, unroll=12):
+    out_ref[:, :, :HD] = (acc[:, :, :HD] * SCALE).astype(jnp.bfloat16)
+    out_ref[:, :, HD:] = acc[:, :, HD:].astype(jnp.bfloat16)
+
+
+def key_grads(counts, tiles, docs, base, kv, qg, stat, unroll=12):
     per, rows = kv.shape[0], total_of(qg)
-    pieces = [*qg, *stat, *carried]
+    pieces = [*qg, *stat]
     spans = [piece[1:] for piece in pieces]
     items = rows * (KB // GROUP) + unroll
     return pl.pallas_call(
-        functools.partial(
-            keys_kernel, unroll, rows, first, gap_at, gap, spans, len(qg), len(stat), len(carried)
-        ),
-        out_shape=blocks(per, jnp.bfloat16 if carried else jnp.float32),
+        functools.partial(keys_kernel, unroll, rows, spans, len(qg)),
+        out_shape=blocks(per, jnp.bfloat16),
         in_specs=[SMEM, SMEM, SMEM, SMEM, VMEM] + [ANYWHERE] * len(pieces),
         out_specs=VMEM,
         scratch_shapes=[
@@ -306,23 +295,41 @@
     return pl.ds(i * HD, HD)
 
 
-def pack_kernel(*refs):
-    *ins, out_ref, sems = refs
-    pairs = []
-    for h in range(out_ref.shape[0]):
-        for j, ref in enumerate(ins):
-            pairs.append((ref.at[:, columns(h)], out_ref.at[h, j // 2, :, columns(j % 2)]))
-    run_copies(pairs, sems)
+def pack_kernel(count, *refs):
+    ins, (out_ref, held, in_sems, sems) = refs[:count], refs[-4:]
+    arrive = [
+        pltpu.make_async_copy(ref, held.at[j], in_sems.at[j]) for j, ref in enumerate(ins)
+    ]
+    for copy in arrive:
+        copy.start()
+    leave = []
+    for j in range(count):
+        arrive[j].wait()
+        for h in range(out_ref.shape[0]):
+            leave.append(
+                pltpu.make_async_copy(
+                    held.at[j, :, columns(h)],
+                    out_ref.at[h, j // 2, :, columns(j % 2)],
+                    sems.at[j, h],
+                )
+            )
+            leave[-1].start()
+    for copy in leave:
+        copy.wait()
 
 
 def to_heads(*arrays):
     heads = arrays[0].shape[1] // HD
     packed = pl.pallas_call(
-        pack_kernel,
+        functools.partial(pack_kernel, len(arrays)),
         out_shape=jax.ShapeDtypeStruct((heads, len(arrays) // 2, BLOCK, 2 * HD), jnp.bfloat16),
         in_specs=[ANYWHERE] * len(arrays),
-        out_specs=VMEM,
-        scratch_shapes=[pltpu.SemaphoreType.DMA((heads * len(arrays),))],
+        out_specs=ANYWHERE,
+        scratch_shapes=[
+            pltpu.VMEM((len(arrays), *arrays[0].shape), jnp.bfloat16),
+            pltpu.SemaphoreType.DMA((len(arrays),)),
+            pltpu.SemaphoreType.DMA((len(arrays), heads)),
+        ],
         name="pack",
     )(*arrays)
     return lax.all_to_all(packed, CORES, 0, 0, tiled=True)
@@ -343,7 +350,7 @@
         unpack_kernel,
         out_shape=(rows, rows),
         in_specs=[VMEM],
-        out_specs=(VMEM, VMEM),
+        out_specs=(ANYWHERE, ANYWHERE),
         scratch_shapes=[pltpu.SemaphoreType.DMA((2 * pair.shape[0],))],
         name="unpack",
     )(pair)
@@ -396,16 +403,11 @@
         tiles, starts, doc_lengths, qg0, 0, half, 0,
         [(kv2, 0, far), *kv1, (kv0, 0, half)], [late, late_stat], [qg2],
     )
-    sums = key_grads(
-        counts, own_tiles, doc_lengths, base, kv0, 0, per, 0,
-        [(qg0, 0, per)], [(stat, 0, per)], [],
-    )
     attended, grad_q = to_tokens(both)
     grads = key_grads(
-        counts, own_tiles, doc_lengths, base, kv0, per, per, 0,
-        [*qg1, (qg2, 0, far)],
-        [(shift(stat, -1), 0, per), (shift(stat, -2), 0, far)],
-        [(sums, 0, per)],
+        counts, own_tiles, doc_lengths, base, kv0,
+        [(qg0, 0, per), *qg1, (qg2, 0, far)],
+        [(stat, 0, per), (shift(stat, -1), 0, per), (shift(stat, -2), 0, far)],
     )
     grad_k, grad_v = to_tokens(grads)
     return attended, grad_q, grad_k, grad_v

time: 164 us -> 163 us (level)
  Pallas kernels: 51.8 us -> 47.5 us
  waiting for transfers between devices: 42 us -> 45.2 us
    pallas_call x3 -> x2, Pallas kernels: 25.6 us -> 22.1 us  [the longest x1 19 us: key_grads(): pl.pallas_call(functools.partial(keys_kernel, unroll, rows, spans, len(qg...]
    ppermute x10, waiting for transfers between devices: 6.46 us -> 9.25 us  [shift(): lax.ppermute(value, 'yz', [(source, source + steps) for source in range(f...]
  transfers between devices with their start and end apart: 14 -> 14, of which waited for: 6 -> 7; matrix products, arithmetic and copies ran while one was open for 3% -> 3% of each run, Pallas kernels for 22% -> 19%
where the time goes in v3:
time: 163 us; the launch traced here: 162 us
  starting transfers between devices  61.7 us (38%)
  Pallas kernels  47.5 us (29%)
  waiting for transfers between devices  45.2 us (28%)
  local copies, waits for them, and re-layouts  6.14 us (4%)
    ppermute x10, starting transfers between devices, shift(): lax.ppermute(value, 'yz', [(source, source + steps) for source in range(f...  41 us
    pallas_call x2, Pallas kernels, attend(): pl.pallas_call(functools.partial(queries_kernel, unroll, first, count, sh...  20.5 us
    all_to_all x1, waiting for transfers between devices, to_heads(): return lax.all_to_all(packed, CORES, 0, 0, tiled=True)  19.6 us
    pallas_call x1, Pallas kernels, key_grads(): pl.pallas_call(functools.partial(keys_kernel, unroll, rows, spans, len(qg...  19 us
    all_to_all x2, waiting for transfers between devices, to_tokens(): pair = lax.all_to_all(pair, CORES, 0, 0, tiled=True)  15.3 us
    all_to_all x2, starting transfers between devices, to_tokens(): pair = lax.all_to_all(pair, CORES, 0, 0, tiled=True)  13.8 us
    ppermute x10, waiting for transfers between devices, shift(): lax.ppermute(value, 'yz', [(source, source + steps) for source in range(f...  9.25 us
    all_to_all x1, starting transfers between devices, to_heads(): return lax.all_to_all(packed, CORES, 0, 0, tiled=True)  6.73 us
  transfers between devices with their start and end apart: 14, of which 7 were waited for; matrix products, arithmetic and copies ran while one was open for 3% of the time, Pallas kernels for 19%

profile of v3, /device:TPU:41, one launch (start us, length us, event | category | flops | bytes accessed | tf_op | source)
XLA Modules:
  0.0 162.1 jit_solution(7620063564977280502)
XLA Ops:
  0.6 3.0 %pack.1 = bf16[16,2,128,256]{3,2,1,0:T(8,128)(2,1)} custom-call(bf16[128,2048]{1,0:T(8,128)(2,1)} %refs_0_.1, bf16[128,2048]{1,0:T(8,128)(2,1)} %refs_1_.1, bf16[128,2048]{1,0:T(8,128)(2,1)} %refs_2_.1, bf16[128,2048]{1,0:T(8,128)(2,1)} %refs_3_.1), custom_call_target="tpu_custom_call" | custom-call | tf_op jit(solution)/shard_map/pack/pallas_call | solution.py:323
  3.7 6.7 %all-to-all-start = ((bf16[16,2,128,256]{3,2,1,0:T(8,128)(2,1)}), bf16[16,2,128,256]{3,2,1,0:T(8,128)(2,1)S(1)}, u32[]{:S(2)}, u32[]{:S(2)}) async-start(bf16[16,2,128,256]{3,2,1,0:T(8,128)(2,1)} %pack.1), calls=%async_computation | async-start | bytes 4194304 | tf_op jit(solution)/shard_map/all_to_all | solution.py:335
  10.4 0.2 collective-permute-start
  10.6 1.1 collective-permute-done
  11.7 1.9 %collective-permute-start.1 = (s32[16,16]{1,0:T(8,128)S(1)}, s32[16,16]{1,0:T(8,128)S(1)}, u32[]{:S(2)}, u32[]{:S(2)}) collective-permute-start(s32[16,16]{1,0:T(8,128)S(1)} %pad_add_fusion.1), channel_id=1, source_target_pairs={{16,0},{32,16},{48,32},{64,48},{80,64},{96,80},{112,96},{128,112},... | collective-permute-start | bytes 3080 | tf_op jit(solution)/shard_map/ppermute | solution.py:362
  13.6 8.5 %collective-permute-start.2 = (s32[7,16]{1,0:T(8,128)S(1)}, s32[7,16]{1,0:T(8,128)S(1)}, u32[]{:S(2)}, u32[]{:S(2)}) collective-permute-start(s32[7,16]{1,0:T(8,128)S(1)} %bitcast.26), channel_id=1, source_target_pairs={{32,0},{48,16},{64,32},{80,48},{96,64},{112,80},{128,96},{144,112}... | collective-permute-start | bytes 1352 | tf_op jit(solution)/shard_map/ppermute | solution.py:362
  22.1 19.6 %all-to-all-done = bf16[16,2,128,256]{3,2,1,0:T(8,128)(2,1)S(1)} async-done(((bf16[16,2,128,256]{3,2,1,0:T(8,128)(2,1)}), bf16[16,2,128,256]{3,2,1,0:T(8,128)(2,1)S(1)}, u32[]{:S(2)}, u32[]{:S(2)}) %all-to-all-start) | async-done | bytes 2097184 | tf_op jit(solution)/shard_map/all_to_all | solution.py:335
  41.8 0.9 slice_bitcast_fusion.4
  42.7 3.5 %collective-permute-start.3 = (bf16[7,128,256]{2,1,0:T(8,128)(2,1)S(1)}, bf16[7,128,256]{2,1,0:T(8,128)(2,1)}, u32[]{:S(2)}, u32[]{:S(2)}) collective-permute-start(bf16[7,128,256]{2,1,0:T(8,128)(2,1)S(1)} %get-tuple-element.26), channel_id=1, source_target_pairs={{0,16},{16,32},{32,48},{48,64},{64,80},{80,96},{96,112},{112,128},... | collective-permute-start | bytes 1376264 | tf_op jit(solution)/shard_map/ppermute | solution.py:362
  46.2 1.9 %collective-permute-start.6 = (bf16[7,128,256]{2,1,0:T(8,128)(2,1)}, bf16[7,128,256]{2,1,0:T(8,128)(2,1)}, u32[]{:S(2)}, u32[]{:S(2)}) collective-permute-start(bf16[7,128,256]{2,1,0:T(8,128)(2,1)} %get-tuple-element.25), channel_id=1, source_target_pairs={{16,0},{32,16},{48,32},{64,48},{80,64},{96,80},{112,96},{128,112},... | collective-permute-start | bytes 1376264 | tf_op jit(solution)/shard_map/ppermute | solution.py:362
  48.3 1.1 slice_bitcast_fusion.2
  49.4 3.5 %collective-permute-start.5 = (bf16[9,128,256]{2,1,0:T(8,128)(2,1)}, bf16[9,128,256]{2,1,0:T(8,128)(2,1)S(1)}, u32[]{:S(2)}, u32[]{:S(2)}) collective-permute-start(bf16[9,128,256]{2,1,0:T(8,128)(2,1)} %get-tuple-element.24), channel_id=1, source_target_pairs={{0,16},{16,32},{32,48},{48,64},{64,80},{80,96},{96,112},{112,128},... | collective-permute-start | bytes 1769480 | tf_op jit(solution)/shard_map/ppermute | solution.py:362
  52.9 4.8 %collective-permute-start.7 = (bf16[9,128,256]{2,1,0:T(8,128)(2,1)}, bf16[9,128,256]{2,1,0:T(8,128)(2,1)S(1)}, u32[]{:S(2)}, u32[]{:S(2)}) collective-permute-start(bf16[9,128,256]{2,1,0:T(8,128)(2,1)} %get-tuple-element.23), channel_id=1, source_target_pairs={{16,0},{32,16},{48,32},{64,48},{80,64},{96,80},{112,96},{128,112},... | collective-permute-start | bytes 1769480 | tf_op jit(solution)/shard_map/ppermute | solution.py:362
  58.0 2.4 %collective-permute-done.6.refs_3_.refs_1_ = bf16[7,128,256]{2,1,0:T(8,128)(2,1)} collective-permute-done((bf16[7,128,256]{2,1,0:T(8,128)(2,1)}, bf16[7,128,256]{2,1,0:T(8,128)(2,1)}, u32[]{:S(2)}, u32[]{:S(2)}) %collective-permute-start.6) | collective-permute-done | bytes 458784 | tf_op jit(solution)/shard_map/ppermute | solution.py:362
  60.4 4.2 %collective-permute-start.8 = (bf16[7,128,256]{2,1,0:T(8,128)(2,1)}, bf16[7,128,256]{2,1,0:T(8,128)(2,1)S(1)}, u32[]{:S(2)}, u32[]{:S(2)}) collective-permute-start(bf16[7,128,256]{2,1,0:T(8,128)(2,1)} %collective-permute-done.6.refs_3_.refs_1_), channel_id=1, source_target_pairs={{16,0},{32,16},{48,32},{64,48},{80,64},{96,80},{112,96},{128,112},... | collective-permute-start | bytes 1376264 | tf_op jit(solution)/shard_map/ppermute | solution.py:362
  64.7 2.6 %collective-permute-start.4 = (bf16[7,128,256]{2,1,0:T(8,128)(2,1)}, bf16[7,128,256]{2,1,0:T(8,128)(2,1)S(1)}, u32[]{:S(2)}, u32[]{:S(2)}) collective-permute-start(bf16[7,128,256]{2,1,0:T(8,128)(2,1)} %collective-permute-done.3.refs_1_.refs_2_), channel_id=1, source_target_pairs={{0,16},{16,32},{32,48},{48,64},{64,80},{80,96},{96,112},{112,128},... | collective-permute-start | bytes 1376264 | tf_op jit(solution)/shard_map/ppermute | solution.py:362
  67.3 1.7 %slice_bitcast_fusion = (bf16[16,128,256]{2,1,0:T(8,128)(2,1)S(1)}, bf16[16,128,256]{2,1,0:T(8,128)(2,1)S(1)}) fusion(bf16[16,2,128,256]{3,2,1,0:T(8,128)(2,1)} %copy-done.4), kind=kLoop, calls=%fused_computation | loop fusion | bytes 4194304 | tf_op jit(solution)/shard_map/squeeze | solution.py:378
  69.0 0.3 collective-permute-done.5.refs_0_.refs_1_
  69.3 3.7 %collective-permute-done.7.refs_4_.refs_2_ = bf16[9,128,256]{2,1,0:T(8,128)(2,1)S(1)} collective-permute-done((bf16[9,128,256]{2,1,0:T(8,128)(2,1)}, bf16[9,128,256]{2,1,0:T(8,128)(2,1)S(1)}, u32[]{:S(2)}, u32[]{:S(2)}) %collective-permute-start.7) | collective-permute-done | bytes 589856 | tf_op jit(solution)/shard_map/ppermute | solution.py:362
  73.0 10.1 %attend.2 = (bf16[8,128,256]{2,1,0:T(8,128)(2,1)S(1)}, f32[8,2,128]{2,1,0:T(2,128)S(1)}) custom-call(s32[16,16]{1,0:T(8,128)S(1)} %get-tuple-element.30.tile_ref, s32[16,16]{1,0:T(8,128)S(1)} %get-tuple-element.29.start_ref, s32[8]{0:T(128)S(1)} %copy-done.3, bf16[16,128,256]{2,1,0:T(8,128)(2,1)S(1)} %get-tuple-element.28.qg_ref.refs_0_, ...), custom_call_target="tpu_custom_call" | custom-call | flops 268435456 | bytes 1048576 | tf_op jit(solution)/shard_map/attend/pallas_call | solution.py:178
  83.1 10.4 %attend.3 = (bf16[16,128,256]{2,1,0:T(8,128)(2,1)S(1)}, f32[16,2,128]{2,1,0:T(2,128)S(1)}) custom-call(s32[16,16]{1,0:T(8,128)S(1)} %get-tuple-element.30.tile_ref, s32[16,16]{1,0:T(8,128)S(1)} %get-tuple-element.29.start_ref, s32[8]{0:T(128)S(1)} %copy-done.3, bf16[16,128,256]{2,1,0:T(8,128)(2,1)S(1)} %get-tuple-element.28.qg_ref.refs_0_, ...), custom_call_target="tpu_custom_call" | custom-call | flops 268435456 | bytes 1048576 | tf_op jit(solution)/shard_map/attend/pallas_call | solution.py:178
  93.6 1.0 copy-done.2
  94.5 6.1 %all-to-all-start.1 = ((bf16[16,128,256]{2,1,0:T(8,128)(2,1)}), bf16[16,128,256]{2,1,0:T(8,128)(2,1)}, u32[]{:S(2)}, u32[]{:S(2)}) async-start(bf16[16,128,256]{2,1,0:T(8,128)(2,1)} %copy-done.2), calls=%async_computation.1 | async-start | bytes 2097152 | tf_op jit(solution)/shard_map/all_to_all | solution.py:347
  101.1 8.0 %collective-permute-start.10 = (f32[16,2,128]{2,1,0:T(2,128)S(1)}, f32[16,2,128]{2,1,0:T(2,128)S(1)}, u32[]{:S(2)}, u32[]{:S(2)}) collective-permute-start(f32[16,2,128]{2,1,0:T(2,128)S(1)} %get-tuple-element.17.refs_4_), channel_id=1, source_target_pairs={{32,0},{48,16},{64,32},{80,48},{96,64},{112,80},{128,96},{144,112}... | collective-permute-start | bytes 49160 | tf_op jit(solution)/shard_map/ppermute | solution.py:362
  109.2 1.9 %collective-permute-start.9 = (f32[16,2,128]{2,1,0:T(2,128)S(1)}, f32[16,2,128]{2,1,0:T(2,128)S(1)}, u32[]{:S(2)}, u32[]{:S(2)}) collective-permute-start(f32[16,2,128]{2,1,0:T(2,128)S(1)} %get-tuple-element.17.refs_4_), channel_id=1, source_target_pairs={{16,0},{32,16},{48,32},{64,48},{80,64},{96,80},{112,96},{128,112},... | collective-permute-start | bytes 49160 | tf_op jit(solution)/shard_map/ppermute | solution.py:362
  111.3 2.8 %collective-permute-done.9.refs_5_ = f32[16,2,128]{2,1,0:T(2,128)S(1)} collective-permute-done((f32[16,2,128]{2,1,0:T(2,128)S(1)}, f32[16,2,128]{2,1,0:T(2,128)S(1)}, u32[]{:S(2)}, u32[]{:S(2)}) %collective-permute-start.9) | collective-permute-done | bytes 16416 | tf_op jit(solution)/shard_map/ppermute | solution.py:362
  114.0 19.0 %key_grads.1 = bf16[16,128,256]{2,1,0:T(8,128)(2,1)} custom-call(s32[39]{0:T(128)S(1)} %get-tuple-element.20.count_ref, s32[39,20]{1,0:T(8,128)S(1)} %copy.52.tile_ref, s32[8]{0:T(128)S(1)} %copy-done.3, s32[1]{0:T(128)} %bitcast.6.base_ref, bf16[16,128,256]{2,1,0:T(8,128)(2,1)S(1)} %get-tuple-element.27.refs_2_.refs_3_.kv_ref, ...), custom_call_target="tpu_custom_call" | custom-call | flops 654311424 | bytes 1048576 | tf_op jit(solution)/shard_map/key_grads/pallas_call | solution.py:264
  133.1 7.6 %all-to-all-start.2 = ((bf16[16,128,256]{2,1,0:T(8,128)(2,1)}), bf16[16,128,256]{2,1,0:T(8,128)(2,1)S(1)}, u32[]{:S(2)}, u32[]{:S(2)}) async-start(bf16[16,128,256]{2,1,0:T(8,128)(2,1)} %key_grads.1), calls=%async_computation.2 | async-start | bytes 2097152 | tf_op jit(solution)/shard_map/all_to_all | solution.py:347
  140.7 2.4 %unpack.2 = (bf16[128,2048]{1,0:T(8,128)(2,1)}, bf16[128,2048]{1,0:T(8,128)(2,1)}) custom-call(bf16[16,128,256]{2,1,0:T(8,128)(2,1)} %all-to-all-done.1.pair_ref), custom_call_target="tpu_custom_call" | custom-call | tf_op jit(solution)/shard_map/unpack/pallas_call | solution.py:349
  143.2 15.3 %all-to-all-done.2.pair_ref = bf16[16,128,256]{2,1,0:T(8,128)(2,1)S(1)} async-done(((bf16[16,128,256]{2,1,0:T(8,128)(2,1)}), bf16[16,128,256]{2,1,0:T(8,128)(2,1)S(1)}, u32[]{:S(2)}, u32[]{:S(2)}) %all-to-all-start.2) | async-done | bytes 1048608 | tf_op jit(solution)/shard_map/all_to_all | solution.py:347
  158.5 1.0 copy-done.5
  159.5 2.4 %unpack.3 = (bf16[128,2048]{1,0:T(8,128)(2,1)}, bf16[128,2048]{1,0:T(8,128)(2,1)}) custom-call(bf16[16,128,256]{2,1,0:T(8,128)(2,1)} %copy-done.5), custom_call_target="tpu_custom_call" | custom-call | tf_op jit(solution)/shard_map/unpack/pallas_call | solution.py:349
  (34 shorter events, 1.0 us)
Async XLA Ops:
  3.7 6.7 %copy-start.6 = (s32[8,16]{1,0:T(8,128)S(1)}, s32[8,16]{1,0:T(8,128)}, u32[]{:S(2)}) copy-start(s32[8,16]{1,0:T(8,128)} %param.10) | copy-start | bytes 1540
  3.7 38.1 %all-to-all-start = ((bf16[16,2,128,256]{3,2,1,0:T(8,128)(2,1)}), bf16[16,2,128,256]{3,2,1,0:T(8,128)(2,1)S(1)}, u32[]{:S(2)}, u32[]{:S(2)}) async-start(bf16[16,2,128,256]{3,2,1,0:T(8,128)(2,1)} %pack.1), calls=%async_computation | async-start | bytes 4194304 | tf_op jit(solution)/shard_map/all_to_all | solution.py:335
  10.4 1.3 collective-permute-start
  11.7 36.5 %collective-permute-start.1 = (s32[16,16]{1,0:T(8,128)S(1)}, s32[16,16]{1,0:T(8,128)S(1)}, u32[]{:S(2)}, u32[]{:S(2)}) collective-permute-start(s32[16,16]{1,0:T(8,128)S(1)} %pad_add_fusion.1), channel_id=1, source_target_pairs={{16,0},{32,16},{48,32},{64,48},{80,64},{96,80},{112,96},{128,112},... | collective-permute-start | bytes 3080 | tf_op jit(solution)/shard_map/ppermute | solution.py:362
  13.6 34.6 %collective-permute-start.2 = (s32[7,16]{1,0:T(8,128)S(1)}, s32[7,16]{1,0:T(8,128)S(1)}, u32[]{:S(2)}, u32[]{:S(2)}) collective-permute-start(s32[7,16]{1,0:T(8,128)S(1)} %bitcast.26), channel_id=1, source_target_pairs={{32,0},{48,16},{64,32},{80,48},{96,64},{112,80},{128,96},{144,112}... | collective-permute-start | bytes 1352 | tf_op jit(solution)/shard_map/ppermute | solution.py:362
  41.8 7.6 %copy-start.4 = (bf16[16,2,128,256]{3,2,1,0:T(8,128)(2,1)}, bf16[16,2,128,256]{3,2,1,0:T(8,128)(2,1)S(1)}, u32[]{:S(2)}) copy-start(bf16[16,2,128,256]{3,2,1,0:T(8,128)(2,1)S(1)} %all-to-all-done) | copy-start | bytes 6291460
  42.7 21.9 %collective-permute-start.3 = (bf16[7,128,256]{2,1,0:T(8,128)(2,1)S(1)}, bf16[7,128,256]{2,1,0:T(8,128)(2,1)}, u32[]{:S(2)}, u32[]{:S(2)}) collective-permute-start(bf16[7,128,256]{2,1,0:T(8,128)(2,1)S(1)} %get-tuple-element.26), channel_id=1, source_target_pairs={{0,16},{16,32},{32,48},{48,64},{64,80},{80,96},{96,112},{112,128},... | collective-permute-start | bytes 1376264 | tf_op jit(solution)/shard_map/ppermute | solution.py:362
  46.2 14.2 %collective-permute-start.6 = (bf16[7,128,256]{2,1,0:T(8,128)(2,1)}, bf16[7,128,256]{2,1,0:T(8,128)(2,1)}, u32[]{:S(2)}, u32[]{:S(2)}) collective-permute-start(bf16[7,128,256]{2,1,0:T(8,128)(2,1)} %get-tuple-element.25), channel_id=1, source_target_pairs={{16,0},{32,16},{48,32},{64,48},{80,64},{96,80},{112,96},{128,112},... | collective-permute-start | bytes 1376264 | tf_op jit(solution)/shard_map/ppermute | solution.py:362
  49.4 19.9 %collective-permute-start.5 = (bf16[9,128,256]{2,1,0:T(8,128)(2,1)}, bf16[9,128,256]{2,1,0:T(8,128)(2,1)S(1)}, u32[]{:S(2)}, u32[]{:S(2)}) collective-permute-start(bf16[9,128,256]{2,1,0:T(8,128)(2,1)} %get-tuple-element.24), channel_id=1, source_target_pairs={{0,16},{16,32},{32,48},{48,64},{64,80},{80,96},{96,112},{112,128},... | collective-permute-start | bytes 1769480 | tf_op jit(solution)/shard_map/ppermute | solution.py:362
  52.9 20.0 %collective-permute-start.7 = (bf16[9,128,256]{2,1,0:T(8,128)(2,1)}, bf16[9,128,256]{2,1,0:T(8,128)(2,1)S(1)}, u32[]{:S(2)}, u32[]{:S(2)}) collective-permute-start(bf16[9,128,256]{2,1,0:T(8,128)(2,1)} %get-tuple-element.23), channel_id=1, source_target_pairs={{16,0},{32,16},{48,32},{64,48},{80,64},{96,80},{112,96},{128,112},... | collective-permute-start | bytes 1769480 | tf_op jit(solution)/shard_map/ppermute | solution.py:362
  60.4 22.7 %collective-permute-start.8 = (bf16[7,128,256]{2,1,0:T(8,128)(2,1)}, bf16[7,128,256]{2,1,0:T(8,128)(2,1)S(1)}, u32[]{:S(2)}, u32[]{:S(2)}) collective-permute-start(bf16[7,128,256]{2,1,0:T(8,128)(2,1)} %collective-permute-done.6.refs_3_.refs_1_), channel_id=1, source_target_pairs={{16,0},{32,16},{48,32},{64,48},{80,64},{96,80},{112,96},{128,112},... | collective-permute-start | bytes 1376264 | tf_op jit(solution)/shard_map/ppermute | solution.py:362
  64.7 18.5 %collective-permute-start.4 = (bf16[7,128,256]{2,1,0:T(8,128)(2,1)}, bf16[7,128,256]{2,1,0:T(8,128)(2,1)S(1)}, u32[]{:S(2)}, u32[]{:S(2)}) collective-permute-start(bf16[7,128,256]{2,1,0:T(8,128)(2,1)} %collective-permute-done.3.refs_1_.refs_2_), channel_id=1, source_target_pairs={{0,16},{16,32},{32,48},{48,64},{64,80},{80,96},{96,112},{112,128},... | collective-permute-start | bytes 1376264 | tf_op jit(solution)/shard_map/ppermute | solution.py:362
  67.3 5.7 %copy-start.3 = (s32[8]{0:T(128)S(1)}, s32[8]{0:T(128)}, u32[]{:S(2)}) copy-start(s32[8]{0:T(128)} %doc_ref.5) | copy-start | bytes 100
  83.1 10.4 %copy-start = (bf16[7,128,256]{2,1,0:T(8,128)(2,1)}, bf16[7,128,256]{2,1,0:T(8,128)(2,1)S(1)}, u32[]{:S(2)}) copy-start(bf16[7,128,256]{2,1,0:T(8,128)(2,1)S(1)} %collective-permute-done.8.refs_6_.refs_3_) | copy-start | bytes 1376260
  93.6 1.0 copy-start.2
  94.5 19.5 %copy-start.1 = (bf16[7,128,256]{2,1,0:T(8,128)(2,1)S(1)}, bf16[7,128,256]{2,1,0:T(8,128)(2,1)}, u32[]{:S(2)}) copy-start(bf16[7,128,256]{2,1,0:T(8,128)(2,1)} %copy-done) | copy-start | bytes 1376260
  94.5 38.5 %all-to-all-start.1 = ((bf16[16,128,256]{2,1,0:T(8,128)(2,1)}), bf16[16,128,256]{2,1,0:T(8,128)(2,1)}, u32[]{:S(2)}, u32[]{:S(2)}) async-start(bf16[16,128,256]{2,1,0:T(8,128)(2,1)} %copy-done.2), calls=%async_computation.1 | async-start | bytes 2097152 | tf_op jit(solution)/shard_map/all_to_all | solution.py:347
  101.1 10.1 %collective-permute-start.10 = (f32[16,2,128]{2,1,0:T(2,128)S(1)}, f32[16,2,128]{2,1,0:T(2,128)S(1)}, u32[]{:S(2)}, u32[]{:S(2)}) collective-permute-start(f32[16,2,128]{2,1,0:T(2,128)S(1)} %get-tuple-element.17.refs_4_), channel_id=1, source_target_pairs={{32,0},{48,16},{64,32},{80,48},{96,64},{112,80},{128,96},{144,112}... | collective-permute-start | bytes 49160 | tf_op jit(solution)/shard_map/ppermute | solution.py:362
  109.2 4.9 %collective-permute-start.9 = (f32[16,2,128]{2,1,0:T(2,128)S(1)}, f32[16,2,128]{2,1,0:T(2,128)S(1)}, u32[]{:S(2)}, u32[]{:S(2)}) collective-permute-start(f32[16,2,128]{2,1,0:T(2,128)S(1)} %get-tuple-element.17.refs_4_), channel_id=1, source_target_pairs={{16,0},{32,16},{48,32},{64,48},{80,64},{96,80},{112,96},{128,112},... | collective-permute-start | bytes 49160 | tf_op jit(solution)/shard_map/ppermute | solution.py:362
  133.1 25.4 %all-to-all-start.2 = ((bf16[16,128,256]{2,1,0:T(8,128)(2,1)}), bf16[16,128,256]{2,1,0:T(8,128)(2,1)S(1)}, u32[]{:S(2)}, u32[]{:S(2)}) async-start(bf16[16,128,256]{2,1,0:T(8,128)(2,1)} %key_grads.1), calls=%async_computation.2 | async-start | bytes 2097152 | tf_op jit(solution)/shard_map/all_to_all | solution.py:347
  158.5 1.0 copy-start.5

commit v4 on v3

--- a/solution.py
+++ b/solution.py
@@ -352,6 +352,7 @@
         in_specs=[VMEM],
         out_specs=(ANYWHERE, ANYWHERE),
         scratch_shapes=[pltpu.SemaphoreType.DMA((2 * pair.shape[0],))],
+        compiler_params=pltpu.CompilerParams(vmem_limit_bytes=8 << 20),
         name="unpack",
     )(pair)
 

time: 163 us -> 162 us (level)
  Pallas kernels: 47.5 us -> 44 us
  local copies, waits for them, and re-layouts: 6.14 us -> 8.36 us
    pallas_call x2, Pallas kernels: 4.9 us -> 2.45 us  [to_tokens(): pl.pallas_call(unpack_kernel, out_shape=(rows, rows), in_specs=[VMEM], ou...]
    unnamed x14 -> x18, local copies, waits for them, and re-layouts: 1.99 us -> 4.06 us
  transfers between devices with their start and end apart: 14 -> 14, of which waited for: 7 -> 7; matrix products, arithmetic and copies ran while one was open for 3% -> 3% of each run, Pallas kernels for 19% -> 18%
where the time goes in v4:
time: 162 us; the launch traced here: 161 us
  starting transfers between devices  61 us (38%)
  waiting for transfers between devices  46.3 us (29%)
  Pallas kernels  44 us (27%)
  local copies, waits for them, and re-layouts  8.36 us (5%)
    ppermute x10, starting transfers between devices, shift(): lax.ppermute(value, 'yz', [(source, source + steps) for source in range(f...  41 us
    pallas_call x2, Pallas kernels, attend(): pl.pallas_call(functools.partial(queries_kernel, unroll, first, count, sh...  20.5 us
    all_to_all x1, waiting for transfers between devices, to_heads(): return lax.all_to_all(packed, CORES, 0, 0, tiled=True)  19.6 us
    pallas_call x1, Pallas kernels, key_grads(): pl.pallas_call(functools.partial(keys_kernel, unroll, rows, spans, len(qg...  18 us
    all_to_all x2, waiting for transfers between devices, to_tokens(): pair = lax.all_to_all(pair, CORES, 0, 0, tiled=True)  16.5 us
    all_to_all x2, starting transfers between devices, to_tokens(): pair = lax.all_to_all(pair, CORES, 0, 0, tiled=True)  13.1 us
    ppermute x10, waiting for transfers between devices, shift(): lax.ppermute(value, 'yz', [(source, source + steps) for source in range(f...  9.13 us
    all_to_all x1, starting transfers between devices, to_heads(): return lax.all_to_all(packed, CORES, 0, 0, tiled=True)  6.73 us
  transfers between devices with their start and end apart: 14, of which 7 were waited for; matrix products, arithmetic and copies ran while one was open for 3% of the time, Pallas kernels for 18%

profile of v4, /device:TPU:41, one launch (start us, length us, event | category | flops | bytes accessed | tf_op | source)
XLA Modules:
  0.0 161.3 jit_solution(1741504292656048944)
XLA Ops:
  0.6 3.0 %pack.1 = bf16[16,2,128,256]{3,2,1,0:T(8,128)(2,1)} custom-call(bf16[128,2048]{1,0:T(8,128)(2,1)} %refs_0_.1, bf16[128,2048]{1,0:T(8,128)(2,1)} %refs_1_.1, bf16[128,2048]{1,0:T(8,128)(2,1)} %refs_2_.1, bf16[128,2048]{1,0:T(8,128)(2,1)} %refs_3_.1), custom_call_target="tpu_custom_call" | custom-call | tf_op jit(solution)/shard_map/pack/pallas_call | solution.py:323
  3.7 6.7 %all-to-all-start = ((bf16[16,2,128,256]{3,2,1,0:T(8,128)(2,1)}), bf16[16,2,128,256]{3,2,1,0:T(8,128)(2,1)S(1)}, u32[]{:S(2)}, u32[]{:S(2)}) async-start(bf16[16,2,128,256]{3,2,1,0:T(8,128)(2,1)} %pack.1), calls=%async_computation | async-start | bytes 4194304 | tf_op jit(solution)/shard_map/all_to_all | solution.py:335
  10.6 1.1 collective-permute-done
  11.7 1.9 %collective-permute-start.1 = (s32[16,16]{1,0:T(8,128)S(1)}, s32[16,16]{1,0:T(8,128)S(1)}, u32[]{:S(2)}, u32[]{:S(2)}) collective-permute-start(s32[16,16]{1,0:T(8,128)S(1)} %pad_add_fusion.1), channel_id=1, source_target_pairs={{16,0},{32,16},{48,32},{64,48},{80,64},{96,80},{112,96},{128,112},... | collective-permute-start | bytes 3080 | tf_op jit(solution)/shard_map/ppermute | solution.py:363
  13.6 8.5 %collective-permute-start.2 = (s32[7,16]{1,0:T(8,128)S(1)}, s32[7,16]{1,0:T(8,128)S(1)}, u32[]{:S(2)}, u32[]{:S(2)}) collective-permute-start(s32[7,16]{1,0:T(8,128)S(1)} %bitcast.26), channel_id=1, source_target_pairs={{32,0},{48,16},{64,32},{80,48},{96,64},{112,80},{128,96},{144,112}... | collective-permute-start | bytes 1352 | tf_op jit(solution)/shard_map/ppermute | solution.py:363
  22.1 19.6 %all-to-all-done = bf16[16,2,128,256]{3,2,1,0:T(8,128)(2,1)S(1)} async-done(((bf16[16,2,128,256]{3,2,1,0:T(8,128)(2,1)}), bf16[16,2,128,256]{3,2,1,0:T(8,128)(2,1)S(1)}, u32[]{:S(2)}, u32[]{:S(2)}) %all-to-all-start) | async-done | bytes 2097184 | tf_op jit(solution)/shard_map/all_to_all | solution.py:335
  41.8 1.1 slice_bitcast_fusion.4
  42.8 3.5 %collective-permute-start.3 = (bf16[7,128,256]{2,1,0:T(8,128)(2,1)}, bf16[7,128,256]{2,1,0:T(8,128)(2,1)}, u32[]{:S(2)}, u32[]{:S(2)}) collective-permute-start(bf16[7,128,256]{2,1,0:T(8,128)(2,1)} %get-tuple-element.26), channel_id=1, source_target_pairs={{0,16},{16,32},{32,48},{48,64},{64,80},{80,96},{96,112},{112,128},... | collective-permute-start | bytes 1376264 | tf_op jit(solution)/shard_map/ppermute | solution.py:363
  46.4 1.9 %collective-permute-start.6 = (bf16[7,128,256]{2,1,0:T(8,128)(2,1)}, bf16[7,128,256]{2,1,0:T(8,128)(2,1)}, u32[]{:S(2)}, u32[]{:S(2)}) collective-permute-start(bf16[7,128,256]{2,1,0:T(8,128)(2,1)} %get-tuple-element.25), channel_id=1, source_target_pairs={{16,0},{32,16},{48,32},{64,48},{80,64},{96,80},{112,96},{128,112},... | collective-permute-start | bytes 1376264 | tf_op jit(solution)/shard_map/ppermute | solution.py:363
  48.4 1.1 slice_bitcast_fusion.2
  49.5 3.5 %collective-permute-start.5 = (bf16[9,128,256]{2,1,0:T(8,128)(2,1)}, bf16[9,128,256]{2,1,0:T(8,128)(2,1)S(1)}, u32[]{:S(2)}, u32[]{:S(2)}) collective-permute-start(bf16[9,128,256]{2,1,0:T(8,128)(2,1)} %get-tuple-element.24), channel_id=1, source_target_pairs={{0,16},{16,32},{32,48},{48,64},{64,80},{80,96},{96,112},{112,128},... | collective-permute-start | bytes 1769480 | tf_op jit(solution)/shard_map/ppermute | solution.py:363
  53.1 4.8 %collective-permute-start.7 = (bf16[9,128,256]{2,1,0:T(8,128)(2,1)}, bf16[9,128,256]{2,1,0:T(8,128)(2,1)S(1)}, u32[]{:S(2)}, u32[]{:S(2)}) collective-permute-start(bf16[9,128,256]{2,1,0:T(8,128)(2,1)} %get-tuple-element.23), channel_id=1, source_target_pairs={{16,0},{32,16},{48,32},{64,48},{80,64},{96,80},{112,96},{128,112},... | collective-permute-start | bytes 1769480 | tf_op jit(solution)/shard_map/ppermute | solution.py:363
  58.2 2.4 %collective-permute-done.6.refs_3_.refs_1_ = bf16[7,128,256]{2,1,0:T(8,128)(2,1)} collective-permute-done((bf16[7,128,256]{2,1,0:T(8,128)(2,1)}, bf16[7,128,256]{2,1,0:T(8,128)(2,1)}, u32[]{:S(2)}, u32[]{:S(2)}) %collective-permute-start.6) | collective-permute-done | bytes 458784 | tf_op jit(solution)/shard_map/ppermute | solution.py:363
  60.6 4.2 %collective-permute-start.8 = (bf16[7,128,256]{2,1,0:T(8,128)(2,1)}, bf16[7,128,256]{2,1,0:T(8,128)(2,1)S(1)}, u32[]{:S(2)}, u32[]{:S(2)}) collective-permute-start(bf16[7,128,256]{2,1,0:T(8,128)(2,1)} %collective-permute-done.6.refs_3_.refs_1_), channel_id=1, source_target_pairs={{16,0},{32,16},{48,32},{64,48},{80,64},{96,80},{112,96},{128,112},... | collective-permute-start | bytes 1376264 | tf_op jit(solution)/shard_map/ppermute | solution.py:363
  64.8 2.6 %collective-permute-start.4 = (bf16[7,128,256]{2,1,0:T(8,128)(2,1)}, bf16[7,128,256]{2,1,0:T(8,128)(2,1)S(1)}, u32[]{:S(2)}, u32[]{:S(2)}) collective-permute-start(bf16[7,128,256]{2,1,0:T(8,128)(2,1)} %collective-permute-done.3.refs_1_.refs_2_), channel_id=1, source_target_pairs={{0,16},{16,32},{32,48},{48,64},{64,80},{80,96},{96,112},{112,128},... | collective-permute-start | bytes 1376264 | tf_op jit(solution)/shard_map/ppermute | solution.py:363
  67.4 1.7 %slice_bitcast_fusion = (bf16[16,128,256]{2,1,0:T(8,128)(2,1)S(1)}, bf16[16,128,256]{2,1,0:T(8,128)(2,1)S(1)}) fusion(bf16[16,2,128,256]{3,2,1,0:T(8,128)(2,1)} %copy-done.7), kind=kLoop, calls=%fused_computation | loop fusion | bytes 4194304 | tf_op jit(solution)/shard_map/squeeze | solution.py:379
  69.5 3.6 %collective-permute-done.7.refs_4_.refs_2_ = bf16[9,128,256]{2,1,0:T(8,128)(2,1)S(1)} collective-permute-done((bf16[9,128,256]{2,1,0:T(8,128)(2,1)}, bf16[9,128,256]{2,1,0:T(8,128)(2,1)S(1)}, u32[]{:S(2)}, u32[]{:S(2)}) %collective-permute-start.7) | collective-permute-done | bytes 589856 | tf_op jit(solution)/shard_map/ppermute | solution.py:363
  73.1 10.1 %attend.2 = (bf16[8,128,256]{2,1,0:T(8,128)(2,1)S(1)}, f32[8,2,128]{2,1,0:T(2,128)S(1)}) custom-call(s32[16,16]{1,0:T(8,128)S(1)} %get-tuple-element.30.tile_ref, s32[16,16]{1,0:T(8,128)S(1)} %get-tuple-element.29.start_ref, s32[8]{0:T(128)S(1)} %copy-done.6, bf16[16,128,256]{2,1,0:T(8,128)(2,1)S(1)} %get-tuple-element.28.qg_ref.refs_0_, ...), custom_call_target="tpu_custom_call" | custom-call | flops 268435456 | bytes 1048576 | tf_op jit(solution)/shard_map/attend/pallas_call | solution.py:178
  83.3 10.4 %attend.3 = (bf16[16,128,256]{2,1,0:T(8,128)(2,1)S(1)}, f32[16,2,128]{2,1,0:T(2,128)S(1)}) custom-call(s32[16,16]{1,0:T(8,128)S(1)} %get-tuple-element.30.tile_ref, s32[16,16]{1,0:T(8,128)S(1)} %get-tuple-element.29.start_ref, s32[8]{0:T(128)S(1)} %copy-done.6, bf16[16,128,256]{2,1,0:T(8,128)(2,1)S(1)} %get-tuple-element.28.qg_ref.refs_0_, ...), custom_call_target="tpu_custom_call" | custom-call | flops 268435456 | bytes 1048576 | tf_op jit(solution)/shard_map/attend/pallas_call | solution.py:178
  93.7 1.0 copy-done.5
  94.7 5.4 %all-to-all-start.1 = ((bf16[16,128,256]{2,1,0:T(8,128)(2,1)}), bf16[16,128,256]{2,1,0:T(8,128)(2,1)S(1)}, u32[]{:S(2)}, u32[]{:S(2)}) async-start(bf16[16,128,256]{2,1,0:T(8,128)(2,1)} %copy-done.5), calls=%async_computation.1 | async-start | bytes 2097152 | tf_op jit(solution)/shard_map/all_to_all | solution.py:347
  100.6 8.0 %collective-permute-start.10 = (f32[16,2,128]{2,1,0:T(2,128)S(1)}, f32[16,2,128]{2,1,0:T(2,128)S(1)}, u32[]{:S(2)}, u32[]{:S(2)}) collective-permute-start(f32[16,2,128]{2,1,0:T(2,128)S(1)} %get-tuple-element.17.refs_4_), channel_id=1, source_target_pairs={{32,0},{48,16},{64,32},{80,48},{96,64},{112,80},{128,96},{144,112}... | collective-permute-start | bytes 49160 | tf_op jit(solution)/shard_map/ppermute | solution.py:363
  108.6 1.9 %collective-permute-start.9 = (f32[16,2,128]{2,1,0:T(2,128)S(1)}, f32[16,2,128]{2,1,0:T(2,128)S(1)}, u32[]{:S(2)}, u32[]{:S(2)}) collective-permute-start(f32[16,2,128]{2,1,0:T(2,128)S(1)} %get-tuple-element.17.refs_4_), channel_id=1, source_target_pairs={{16,0},{32,16},{48,32},{64,48},{80,64},{96,80},{112,96},{128,112},... | collective-permute-start | bytes 49160 | tf_op jit(solution)/shard_map/ppermute | solution.py:363
  110.7 2.7 %collective-permute-done.9.refs_5_ = f32[16,2,128]{2,1,0:T(2,128)S(1)} collective-permute-done((f32[16,2,128]{2,1,0:T(2,128)S(1)}, f32[16,2,128]{2,1,0:T(2,128)S(1)}, u32[]{:S(2)}, u32[]{:S(2)}) %collective-permute-start.9) | collective-permute-done | bytes 16416 | tf_op jit(solution)/shard_map/ppermute | solution.py:363
  113.3 1.1 copy-done.2
  114.4 1.0 copy-done.4
  115.4 18.0 %key_grads.1 = bf16[16,128,256]{2,1,0:T(8,128)(2,1)S(1)} custom-call(s32[39]{0:T(128)S(1)} %get-tuple-element.20.count_ref, s32[39,20]{1,0:T(8,128)S(1)} %copy.52.tile_ref, s32[8]{0:T(128)S(1)} %copy-done.6, s32[1]{0:T(128)} %bitcast.6.base_ref, bf16[16,128,256]{2,1,0:T(8,128)(2,1)S(1)} %get-tuple-element.27.refs_2_.refs_3_.kv_ref, ...), custom_call_target="tpu_custom_call" | custom-call | flops 654311424 | bytes 1048576 | tf_op jit(solution)/shard_map/key_grads/pallas_call | solution.py:264
  133.5 1.0 copy-done
  134.5 7.7 %all-to-all-start.2 = ((bf16[16,128,256]{2,1,0:T(8,128)(2,1)}), bf16[16,128,256]{2,1,0:T(8,128)(2,1)S(1)}, u32[]{:S(2)}, u32[]{:S(2)}) async-start(bf16[16,128,256]{2,1,0:T(8,128)(2,1)} %copy-done), calls=%async_computation.2 | async-start | bytes 2097152 | tf_op jit(solution)/shard_map/all_to_all | solution.py:347
  142.2 1.2 unpack.2
  143.4 16.5 %all-to-all-done.2.pair_ref = bf16[16,128,256]{2,1,0:T(8,128)(2,1)S(1)} async-done(((bf16[16,128,256]{2,1,0:T(8,128)(2,1)}), bf16[16,128,256]{2,1,0:T(8,128)(2,1)S(1)}, u32[]{:S(2)}, u32[]{:S(2)}) %all-to-all-start.2) | async-done | bytes 1048608 | tf_op jit(solution)/shard_map/all_to_all | solution.py:347
  159.9 1.2 unpack.3
  (38 shorter events, 1.6 us)
Async XLA Ops:
  3.7 6.7 %copy-start.8 = (s32[8,16]{1,0:T(8,128)S(1)}, s32[8,16]{1,0:T(8,128)}, u32[]{:S(2)}) copy-start(s32[8,16]{1,0:T(8,128)} %param.10) | copy-start | bytes 1540
  3.7 38.1 %all-to-all-start = ((bf16[16,2,128,256]{3,2,1,0:T(8,128)(2,1)}), bf16[16,2,128,256]{3,2,1,0:T(8,128)(2,1)S(1)}, u32[]{:S(2)}, u32[]{:S(2)}) async-start(bf16[16,2,128,256]{3,2,1,0:T(8,128)(2,1)} %pack.1), calls=%async_computation | async-start | bytes 4194304 | tf_op jit(solution)/shard_map/all_to_all | solution.py:335
  10.4 1.3 collective-permute-start
  11.7 36.7 %collective-permute-start.1 = (s32[16,16]{1,0:T(8,128)S(1)}, s32[16,16]{1,0:T(8,128)S(1)}, u32[]{:S(2)}, u32[]{:S(2)}) collective-permute-start(s32[16,16]{1,0:T(8,128)S(1)} %pad_add_fusion.1), channel_id=1, source_target_pairs={{16,0},{32,16},{48,32},{64,48},{80,64},{96,80},{112,96},{128,112},... | collective-permute-start | bytes 3080 | tf_op jit(solution)/shard_map/ppermute | solution.py:363
  13.6 34.7 %collective-permute-start.2 = (s32[7,16]{1,0:T(8,128)S(1)}, s32[7,16]{1,0:T(8,128)S(1)}, u32[]{:S(2)}, u32[]{:S(2)}) collective-permute-start(s32[7,16]{1,0:T(8,128)S(1)} %bitcast.26), channel_id=1, source_target_pairs={{32,0},{48,16},{64,32},{80,48},{96,64},{112,80},{128,96},{144,112}... | collective-permute-start | bytes 1352 | tf_op jit(solution)/shard_map/ppermute | solution.py:363
  41.8 25.6 %copy-start.7 = (bf16[16,2,128,256]{3,2,1,0:T(8,128)(2,1)}, bf16[16,2,128,256]{3,2,1,0:T(8,128)(2,1)S(1)}, u32[]{:S(2)}) copy-start(bf16[16,2,128,256]{3,2,1,0:T(8,128)(2,1)S(1)} %all-to-all-done) | copy-start | bytes 6291460
  42.8 21.9 %collective-permute-start.3 = (bf16[7,128,256]{2,1,0:T(8,128)(2,1)}, bf16[7,128,256]{2,1,0:T(8,128)(2,1)}, u32[]{:S(2)}, u32[]{:S(2)}) collective-permute-start(bf16[7,128,256]{2,1,0:T(8,128)(2,1)} %get-tuple-element.26), channel_id=1, source_target_pairs={{0,16},{16,32},{32,48},{48,64},{64,80},{80,96},{96,112},{112,128},... | collective-permute-start | bytes 1376264 | tf_op jit(solution)/shard_map/ppermute | solution.py:363
  46.4 14.2 %collective-permute-start.6 = (bf16[7,128,256]{2,1,0:T(8,128)(2,1)}, bf16[7,128,256]{2,1,0:T(8,128)(2,1)}, u32[]{:S(2)}, u32[]{:S(2)}) collective-permute-start(bf16[7,128,256]{2,1,0:T(8,128)(2,1)} %get-tuple-element.25), channel_id=1, source_target_pairs={{16,0},{32,16},{48,32},{64,48},{80,64},{96,80},{112,96},{128,112},... | collective-permute-start | bytes 1376264 | tf_op jit(solution)/shard_map/ppermute | solution.py:363
  49.5 20.0 %collective-permute-start.5 = (bf16[9,128,256]{2,1,0:T(8,128)(2,1)}, bf16[9,128,256]{2,1,0:T(8,128)(2,1)S(1)}, u32[]{:S(2)}, u32[]{:S(2)}) collective-permute-start(bf16[9,128,256]{2,1,0:T(8,128)(2,1)} %get-tuple-element.24), channel_id=1, source_target_pairs={{0,16},{16,32},{32,48},{48,64},{64,80},{80,96},{96,112},{112,128},... | collective-permute-start | bytes 1769480 | tf_op jit(solution)/shard_map/ppermute | solution.py:363
  53.1 20.0 %collective-permute-start.7 = (bf16[9,128,256]{2,1,0:T(8,128)(2,1)}, bf16[9,128,256]{2,1,0:T(8,128)(2,1)S(1)}, u32[]{:S(2)}, u32[]{:S(2)}) collective-permute-start(bf16[9,128,256]{2,1,0:T(8,128)(2,1)} %get-tuple-element.23), channel_id=1, source_target_pairs={{16,0},{32,16},{48,32},{64,48},{80,64},{96,80},{112,96},{128,112},... | collective-permute-start | bytes 1769480 | tf_op jit(solution)/shard_map/ppermute | solution.py:363
  60.6 22.7 %collective-permute-start.8 = (bf16[7,128,256]{2,1,0:T(8,128)(2,1)}, bf16[7,128,256]{2,1,0:T(8,128)(2,1)S(1)}, u32[]{:S(2)}, u32[]{:S(2)}) collective-permute-start(bf16[7,128,256]{2,1,0:T(8,128)(2,1)} %collective-permute-done.6.refs_3_.refs_1_), channel_id=1, source_target_pairs={{16,0},{32,16},{48,32},{64,48},{80,64},{96,80},{112,96},{128,112},... | collective-permute-start | bytes 1376264 | tf_op jit(solution)/shard_map/ppermute | solution.py:363
  64.8 18.5 %collective-permute-start.4 = (bf16[7,128,256]{2,1,0:T(8,128)(2,1)}, bf16[7,128,256]{2,1,0:T(8,128)(2,1)S(1)}, u32[]{:S(2)}, u32[]{:S(2)}) collective-permute-start(bf16[7,128,256]{2,1,0:T(8,128)(2,1)} %collective-permute-done.3.refs_1_.refs_2_), channel_id=1, source_target_pairs={{0,16},{16,32},{32,48},{48,64},{64,80},{80,96},{96,112},{112,128},... | collective-permute-start | bytes 1376264 | tf_op jit(solution)/shard_map/ppermute | solution.py:363
  67.4 5.7 %copy-start.6 = (s32[8]{0:T(128)S(1)}, s32[8]{0:T(128)}, u32[]{:S(2)}) copy-start(s32[8]{0:T(128)} %doc_ref.5) | copy-start | bytes 100
  73.1 10.1 %copy-start.1 = (bf16[9,128,256]{2,1,0:T(8,128)(2,1)}, bf16[9,128,256]{2,1,0:T(8,128)(2,1)S(1)}, u32[]{:S(2)}) copy-start(bf16[9,128,256]{2,1,0:T(8,128)(2,1)S(1)} %collective-permute-done.7.refs_4_.refs_2_) | copy-start | bytes 1769476
  83.3 10.4 %copy-start.3 = (bf16[7,128,256]{2,1,0:T(8,128)(2,1)}, bf16[7,128,256]{2,1,0:T(8,128)(2,1)S(1)}, u32[]{:S(2)}) copy-start(bf16[7,128,256]{2,1,0:T(8,128)(2,1)S(1)} %collective-permute-done.8.refs_6_.refs_3_) | copy-start | bytes 1376260
  93.7 1.0 copy-start.5
  94.7 39.7 %all-to-all-start.1 = ((bf16[16,128,256]{2,1,0:T(8,128)(2,1)}), bf16[16,128,256]{2,1,0:T(8,128)(2,1)S(1)}, u32[]{:S(2)}, u32[]{:S(2)}) async-start(bf16[16,128,256]{2,1,0:T(8,128)(2,1)} %copy-done.5), calls=%async_computation.1 | async-start | bytes 2097152 | tf_op jit(solution)/shard_map/all_to_all | solution.py:347
  100.6 10.1 %collective-permute-start.10 = (f32[16,2,128]{2,1,0:T(2,128)S(1)}, f32[16,2,128]{2,1,0:T(2,128)S(1)}, u32[]{:S(2)}, u32[]{:S(2)}) collective-permute-start(f32[16,2,128]{2,1,0:T(2,128)S(1)} %get-tuple-element.17.refs_4_), channel_id=1, source_target_pairs={{32,0},{48,16},{64,32},{80,48},{96,64},{112,80},{128,96},{144,112}... | collective-permute-start | bytes 49160 | tf_op jit(solution)/shard_map/ppermute | solution.py:363
  108.6 4.8 %collective-permute-start.9 = (f32[16,2,128]{2,1,0:T(2,128)S(1)}, f32[16,2,128]{2,1,0:T(2,128)S(1)}, u32[]{:S(2)}, u32[]{:S(2)}) collective-permute-start(f32[16,2,128]{2,1,0:T(2,128)S(1)} %get-tuple-element.17.refs_4_), channel_id=1, source_target_pairs={{16,0},{32,16},{48,32},{64,48},{80,64},{96,80},{112,96},{128,112},... | collective-permute-start | bytes 49160 | tf_op jit(solution)/shard_map/ppermute | solution.py:363
  113.3 1.1 copy-start.2
  114.4 1.0 copy-start.4
  133.5 1.0 copy-start
  134.5 25.5 %all-to-all-start.2 = ((bf16[16,128,256]{2,1,0:T(8,128)(2,1)}), bf16[16,128,256]{2,1,0:T(8,128)(2,1)S(1)}, u32[]{:S(2)}, u32[]{:S(2)}) async-start(bf16[16,128,256]{2,1,0:T(8,128)(2,1)} %copy-done), calls=%async_computation.2 | async-start | bytes 2097152 | tf_op jit(solution)/shard_map/all_to_all | solution.py:347
